TPU v7x, 512 devices: a whole 4x8x8 slice. The times are simulated.
512 devices in a mesh: context: 64 (over y, z), tensor: 8 (over x, core).
Axes of the slice: x: 4, y: 8, z: 8, core: 2. Of those that a mesh axis runs over, the one named last changes fastest.
Arguments:
- queries: bfloat16 [8192, 4096], P('context', 'tensor'), may hold values from -6 to 6
- key_gate: bfloat16 [8192, 4096], P('context', 'tensor'), may hold values from -6 to 6
- values: bfloat16 [8192, 4096], P('context', 'tensor'), may hold values from -6 to 6
- residues: float32 [16, 4096], P(None, 'tensor'), may hold values from -0.0625 to 0.0625
- decay_rates: float32 [16, 4096], P(None, 'tensor'), may hold values from 1 to 256
- out_weight: bfloat16 [4096, 4096], P('tensor'), may hold values from -0.09375 to 0.09375
Outputs:
- mixed_rows: bfloat16 [8192, 4096], P('context', 'tensor')
All inputs are finite; a program needn't handle non-finite values.
Results may differ from a plain program's by a relative error of at most 0.024.
Values may be sent and summed in bfloat16 or wider, within the bound.
No kernel may reach another device: no remote copies, remote signals or barrier semaphores. Data moves between devices by JAX's collectives and lax.ppermute only.
A program may use at most 64 MiB of HBM per device.

v0:
```python
import math

import jax
import jax.numpy as jnp
from jax import lax
from jax.sharding import PartitionSpec as P

table_prec = lax.Precision.HIGH


def matmul(left, right):
    return jnp.dot(left, right, precision=table_prec, preferred_element_type=jnp.float32)


def dft_tables(length):
    counter = jnp.arange(length, dtype=jnp.int32)
    phases = counter[:, None] * counter[None, :] % length
    angles = phases.astype(jnp.float32) * (2.0 * math.pi / length)
    return (jnp.cos(angles), jnp.sin(angles))


def forward_dft(tables, real_part, imag_part):
    cosine, sines = tables
    return (
        matmul(cosine, real_part) + matmul(sines, imag_part),
        matmul(cosine, imag_part) - matmul(sines, real_part),
    )


def inverse_dft(tables, real_part, imag_part):
    cosine, sines = tables
    return (
        matmul(cosine, real_part) - matmul(sines, imag_part),
        matmul(cosine, imag_part) + matmul(sines, real_part),
    )


def filter_spectrum(residues, decay_rates, my_block, block_count, row_count, seq_len):
    channels = residues.shape[1]
    step_index = jnp.arange(row_count, dtype=jnp.int32)[:, None, None]
    branch = jnp.arange(2, dtype=jnp.int32)[None, :, None]
    frequency = 2 * (my_block + block_count * step_index) + branch
    angles = frequency.astype(jnp.float32) * (math.pi / seq_len)
    half_sin = jnp.sin(0.5 * angles)
    full_sin = jnp.sin(angles)
    parity = 1.0 - 2.0 * branch.astype(jnp.float32)
    spec_real = jnp.zeros((row_count, 2, channels), jnp.float32)
    spec_imag = jnp.zeros((row_count, 2, channels), jnp.float32)
    for pole_index in range(residues.shape[0]):
        rate_pos = decay_rates[pole_index] / seq_len
        shrink = jnp.exp(-rate_pos)
        denom_real = -jnp.expm1(-rate_pos) + 2.0 * shrink * half_sin * half_sin
        denom_imag = shrink * full_sin
        weight_pole = residues[pole_index] * (1.0 - parity * jnp.exp(-decay_rates[pole_index]))
        weight_pole = weight_pole / (denom_real * denom_real + denom_imag * denom_imag)
        spec_real = spec_real + weight_pole * denom_real
        spec_imag = spec_imag - weight_pole * denom_imag
    return (spec_real, spec_imag)


def spectral_conv(signal, residues, decay_rates):
    row_count, channels = signal.shape
    block_count = lax.axis_size("context")
    my_block = lax.axis_index("context")
    piece_rows = row_count // block_count
    seq_len = row_count * block_count
    spread = lax.all_to_all(
        signal.reshape(1, row_count, channels), "context", split_axis=1, concat_axis=0, tiled=True
    )
    values_in = spread.astype(jnp.float32)
    src_index = jnp.arange(block_count, dtype=jnp.int32)[:, None]
    row_index = my_block * piece_rows + jnp.arange(piece_rows, dtype=jnp.int32)[None, :]
    positions = src_index * row_count + row_index
    twist_angle = positions.astype(jnp.float32) * (math.pi / seq_len)
    twist_cos = jnp.cos(twist_angle)[:, :, None]
    twist_sin = jnp.sin(twist_angle)[:, :, None]
    real_part = jnp.stack([values_in, values_in * twist_cos], axis=2)
    imag_part = jnp.stack([jnp.zeros_like(values_in), -values_in * twist_sin], axis=2)
    flat_shape = (block_count, piece_rows * 2 * channels)
    block_tables = dft_tables(block_count)
    real_part, imag_part = forward_dft(
        block_tables, real_part.reshape(flat_shape), imag_part.reshape(flat_shape)
    )
    real_part = real_part.reshape(block_count, piece_rows, 2, channels)
    imag_part = imag_part.reshape(block_count, piece_rows, 2, channels)
    freq_index = jnp.arange(block_count, dtype=jnp.int32)[:, None]
    phases = freq_index * row_index % seq_len
    angles = phases.astype(jnp.float32) * (2.0 * math.pi / seq_len)
    fwd_cos = jnp.cos(angles)[:, :, None, None]
    fwd_sin = jnp.sin(angles)[:, :, None, None]
    real_part, imag_part = (
        real_part * fwd_cos + imag_part * fwd_sin,
        imag_part * fwd_cos - real_part * fwd_sin,
    )
    packed = jnp.stack([real_part, imag_part], axis=2)
    columns = lax.all_to_all(
        packed.astype(jnp.bfloat16), "context", split_axis=0, concat_axis=1, tiled=True
    ).astype(packed.dtype)
    row_tables = dft_tables(row_count)
    real_part = columns[0, :, 0].reshape(row_count, 2 * channels)
    imag_part = columns[0, :, 1].reshape(row_count, 2 * channels)
    real_part, imag_part = forward_dft(row_tables, real_part, imag_part)
    real_part = real_part.reshape(row_count, 2, channels)
    imag_part = imag_part.reshape(row_count, 2, channels)
    spec_real, spec_imag = filter_spectrum(
        residues, decay_rates, my_block, block_count, row_count, seq_len
    )
    prod_real = real_part * spec_real - imag_part * spec_imag
    prod_imag = real_part * spec_imag + imag_part * spec_real
    real_part, imag_part = inverse_dft(
        row_tables,
        prod_real.reshape(row_count, 2 * channels),
        prod_imag.reshape(row_count, 2 * channels),
    )
    real_part = real_part.reshape(row_count, 2, channels)
    imag_part = imag_part.reshape(row_count, 2, channels)
    time_index = jnp.arange(row_count, dtype=jnp.int32)[:, None, None]
    phases = time_index * my_block % seq_len
    angles = phases.astype(jnp.float32) * (2.0 * math.pi / seq_len)
    inv_cos = jnp.cos(angles)
    inv_sin = jnp.sin(angles)
    real_part, imag_part = (
        real_part * inv_cos - imag_part * inv_sin,
        imag_part * inv_cos + real_part * inv_sin,
    )
    packed = jnp.stack([real_part, imag_part], axis=1).reshape(
        1, block_count, piece_rows, 2, 2, channels
    )
    returned = lax.all_to_all(
        packed.astype(jnp.bfloat16), "context", split_axis=1, concat_axis=0, tiled=True
    ).astype(packed.dtype)
    real_part = returned[:, 0, :, 0].reshape(flat_shape)
    imag_part = returned[:, 0, :, 1].reshape(flat_shape)
    real_part, imag_part = inverse_dft(block_tables, real_part, imag_part)
    real_part = real_part.reshape(block_count, piece_rows, 2, channels)
    imag_part = imag_part.reshape(block_count, piece_rows, 2, channels)
    combined = real_part[:, :, 0] + twist_cos * real_part[:, :, 1] - twist_sin * imag_part[:, :, 1]
    combined = combined / (2.0 * seq_len)
    settled = lax.all_to_all(
        combined.astype(jnp.bfloat16), "context", split_axis=0, concat_axis=1, tiled=True
    ).astype(combined.dtype)
    return settled.reshape(row_count, channels)


def on_device(queries, key_gate, values, residues, decay_rates, out_weight):
    product = (key_gate.astype(jnp.float32) * values.astype(jnp.float32)).astype(jnp.bfloat16)
    convolved = spectral_conv(product, residues, decay_rates)
    gated_rows = (queries.astype(jnp.float32) * convolved).astype(jnp.bfloat16)
    partial_value = jnp.dot(gated_rows, out_weight, preferred_element_type=jnp.float32)
    summed = lax.psum(partial_value.astype(jnp.bfloat16), "tensor").astype(jnp.float32)
    channels = gated_rows.shape[1]
    summed = lax.dynamic_slice_in_dim(summed, lax.axis_index("tensor") * channels, channels, 1)
    return summed.astype(jnp.bfloat16)


def solution(mesh):
    in_specs = (
        P("context", "tensor"),
        P("context", "tensor"),
        P("context", "tensor"),
        P(None, "tensor"),
        P(None, "tensor"),
        P("tensor", None),
    )
    out_specs = P("context", "tensor")
    return jax.shard_map(
        on_device, mesh=mesh, in_specs=in_specs, out_specs=out_specs, check_vma=False
    )
```

profile of v0, /device:TPU:1, one launch (start us, length us, event | category | flops | bytes accessed | tf_op | source)
XLA Modules:
  0.0 205.7 jit_solution(6613810881090930208)
XLA Ops:
  6.5 1.0 fusion.23
  7.7 0.5 broadcast.1639
  8.3 1.4 reduce
  9.7 0.7 reshape.1906
  10.4 17.1 %all-to-all-start = ((bf16[64,2,512]{2,1,0:T(2,128)(2,1)}), bf16[64,2,512]{2,1,0:T(2,128)(2,1)S(1)}, u32[]{:S(2)}, u32[]{:S(2)}) async-start(bf16[64,2,512]{2,1,0:T(2,128)(2,1)} %reshape.1906), calls=%async_computation | async-start | bytes 262144 | tf_op jit(solution)/shard_map/all_to_all | solution.py:67
  27.5 1.1 negate_exponential_fusion.14
  28.7 1.1 negate_exponential_fusion.15
  29.8 1.0 negate_exponential_fusion.13
  31.2 1.2 fusion.159
  33.3 5.7 %all-to-all-done = bf16[64,2,512]{2,1,0:T(2,128)(2,1)S(1)} async-done(((bf16[64,2,512]{2,1,0:T(2,128)(2,1)}), bf16[64,2,512]{2,1,0:T(2,128)(2,1)S(1)}, u32[]{:S(2)}, u32[]{:S(2)}) %all-to-all-start) | async-done | bytes 131104 | tf_op jit(solution)/shard_map/all_to_all | solution.py:67
  40.8 0.5 fusion.58
  42.0 0.5 fusion.56
  42.5 0.5 convolution_add_fusion.1
  43.5 0.5 convolution_subtract_fusion.1
  44.8 1.3 copy.51
  46.2 6.4 %all-to-all-start.1 = ((bf16[64,2,2,2,512]{4,3,1,2,0:T(2,128)(2,1)}), bf16[64,2,2,2,512]{4,3,1,2,0:T(2,128)(2,1)S(1)}, u32[]{:S(2)}, u32[]{:S(2)}) async-start(bf16[64,2,2,2,512]{4,3,1,2,0:T(2,128)(2,1)} %copy.51), calls=%async_computation.1 | async-start | bytes 1048576 | tf_op jit(solution)/shard_map/all_to_all | solution.py:96
  55.0 13.6 %all-to-all-done.1 = bf16[64,2,2,2,512]{4,3,1,2,0:T(2,128)(2,1)S(1)} async-done(((bf16[64,2,2,2,512]{4,3,1,2,0:T(2,128)(2,1)}), bf16[64,2,2,2,512]{4,3,1,2,0:T(2,128)(2,1)S(1)}, u32[]{:S(2)}, u32[]{:S(2)}) %all-to-all-start.1) | async-done | bytes 524320 | tf_op jit(solution)/shard_map/all_to_all | solution.py:96
  69.3 0.5 fusion.41
  69.9 0.5 fusion.39
  70.4 0.5 convolution_add_fusion.3
  71.0 4.7 %multiply_add_fusion = (f32[128,1024]{1,0:T(8,128)S(1)}, f32[128,1024]{1,0:T(8,128)S(1)}, f32[128,1024]{1,0:T(8,128)S(1)}, f32[128,1024]{1,0:T(8,128)S(1)}) fusion(f32[128,1024]{1,0:T(8,128)S(1)} %convolution_add_fusion.3, f32[128,1024]{1,0:T(8,128)S(1)} %bitcast.390, f32[1024]{0:T(1024)S(1)} %bitcast.535, f32[128,1024]{1,0:T(8,128)S(1)} %bitcast.389, ...), kind=kOutput, calls=%fused_computation.46 | convolution fusion | flops 126451712 | bytes 4718592 | tf_op jit(solution)/shard_map/dot_general | solution.py:12
  75.9 0.6 fusion.37
  76.5 0.6 fusion.35
  77.1 0.6 convolution_subtract_fusion.2
  78.2 0.6 convolution_add_fusion.2
  79.3 0.9 fusion.20
  80.2 0.7 pad_maximum_fusion.2
  80.8 22.9 %all_to_all.42 = bf16[1,64,2,2,2,512]{5,4,2,3,0,1:T(2,128)(2,1)S(1)} all-to-all(bf16[1,64,2,2,2,512]{5,4,2,3,0,1:T(2,128)(2,1)S(1)} %pad_maximum_fusion.2), channel_id=1, replica_groups=mesh['context'=64,'tensor'=8] {'context'}, dimensions={1} | all-to-all | bytes 1048576 | tf_op jit(solution)/shard_map/all_to_all | solution.py:129
  108.2 19.7 %all_to_all.43 = bf16[64,2,512]{2,1,0:T(2,128)(2,1)S(1)} all-to-all(bf16[64,2,512]{2,1,0:T(2,128)(2,1)S(1)} %fusion.22), channel_id=1, replica_groups=mesh['context'=64,'tensor'=8] {'context'}, dimensions={0} | all-to-all | bytes 262144 | tf_op jit(solution)/shard_map/all_to_all | solution.py:139
  127.9 3.9 %convolution_convert_fusion = bf16[128,4096]{1,0:T(8,128)(2,1)} fusion(bf16[512,4096]{1,0:T(8,128)(2,1)} %param.11, f32[128,512]{1,0:T(8,128)S(1)} %reshape.1905, bf16[128,512]{1,0:T(8,128)(2,1)S(1)} %copy-done), kind=kOutput, calls=%fused_computation | convolution fusion | flops 537591808 | bytes 5636096 | tf_op jit(solution)/shard_map/dot_general | solution.py:149
  131.8 65.4 %all-reduce.3.cloned.1.call-done = bf16[128,4096]{1,0:T(8,128)(2,1)} async-done(((bf16[128,4096]{1,0:T(8,128)(2,1)}), bf16[128,4096]{1,0:T(8,128)(2,1)}) %all-reduce.3.cloned.1.call-update) | async-done | bytes 1048592 | tf_op jit(solution)/shard_map/psum | solution.py:150
  197.3 1.6 convert_convert_fusion
  (232 shorter events, 12.4 us)
Async XLA Ops:
  10.4 28.6 %all-to-all-start = ((bf16[64,2,512]{2,1,0:T(2,128)(2,1)}), bf16[64,2,512]{2,1,0:T(2,128)(2,1)S(1)}, u32[]{:S(2)}, u32[]{:S(2)}) async-start(bf16[64,2,512]{2,1,0:T(2,128)(2,1)} %reshape.1906), calls=%async_computation | async-start | bytes 262144 | tf_op jit(solution)/shard_map/all_to_all | solution.py:67
  46.2 22.4 %all-to-all-start.1 = ((bf16[64,2,2,2,512]{4,3,1,2,0:T(2,128)(2,1)}), bf16[64,2,2,2,512]{4,3,1,2,0:T(2,128)(2,1)S(1)}, u32[]{:S(2)}, u32[]{:S(2)}) async-start(bf16[64,2,2,2,512]{4,3,1,2,0:T(2,128)(2,1)} %copy.51), calls=%async_computation.1 | async-start | bytes 1048576 | tf_op jit(solution)/shard_map/all_to_all | solution.py:96
  52.6 144.7 %all-reduce.3.cloned.1.call-start = ((), (), s32[]{:S(2)}) async-start(), calls=%async_computation.4 | async-start | bytes 2097152 | tf_op jit(solution)/shard_map/psum | solution.py:150
  104.9 23.0 %copy-start = (bf16[128,512]{1,0:T(8,128)(2,1)S(1)}, bf16[128,512]{1,0:T(8,128)(2,1)}, u32[]{:S(2)}) copy-start(bf16[128,512]{1,0:T(8,128)(2,1)} %param.6) | copy-start | bytes 393220
Sparse Core Ops, SparseCore 0:
  132.0 65.2 all-reduce.2
where the time goes:
time: 207 us; the launch traced here: 206 us
  waiting for transfers between devices  84.7 us (41%)
  blocking collectives  42.6 us (21%)
  starting transfers between devices  23.8 us (11%)
  matrix products  16.3 us (8%)
  between operations  15.3 us (7%)
  local copies, waits for them, and re-layouts  11.8 us (6%)
  other arithmetic  11.2 us (5%)
    psum x1, waiting for transfers between devices, on_device(): lax.psum(partial_value.astype(jnp.bfloat16), 'tensor').astype(jnp.float32)  65.4 us
    all_to_all x1, blocking collectives, spectral_conv(): lax.all_to_all(packed.astype(jnp.bfloat16), 'context', split_axis=1, conc...  22.9 us
    all_to_all x1, blocking collectives, spectral_conv(): lax.all_to_all(combined.astype(jnp.bfloat16), 'context', split_axis=0, co...  19.7 us
    all_to_all x1, starting transfers between devices, spectral_conv(): lax.all_to_all(signal.reshape(1, row_count, channels), 'context', split_a...  17.1 us
    all_to_all x1, waiting for transfers between devices, spectral_conv(): lax.all_to_all(packed.astype(jnp.bfloat16), 'context', split_axis=0, conc...  13.6 us
    dot_general x16, matrix products, matmul(): jnp.dot(left, right, precision=table_prec, preferred_element_type=jnp.flo...  12.4 us
    all_to_all x1, starting transfers between devices, spectral_conv(): lax.all_to_all(packed.astype(jnp.bfloat16), 'context', split_axis=0, conc...  6.44 us
    all_to_all x1, waiting for transfers between devices, spectral_conv(): lax.all_to_all(signal.reshape(1, row_count, channels), 'context', split_a...  5.71 us
  transfers between devices with their start and end apart: 3, of which 3 were waited for; matrix products, arithmetic and copies ran while one was open for 3% of the time, Pallas kernels for 0%

commit v1 on v0

v1 whole, which is shorter than its diff:
```python
import jax
import jax.numpy as jnp
from jax import lax
from jax.experimental import pallas as pl
from jax.experimental.pallas import tpu as pltpu
from jax.sharding import PartitionSpec as P

SEQ = 8192
POLES = 16
ROWS = 128
CHANNELS = 512
LANES = 128
SUBS = 8
STEPS = ROWS // SUBS
RING = 8
XCHIPS = 4
LINK = jnp.bfloat16

GROUPS = tuple(slice(g * LANES, (g + 1) * LANES) for g in range(CHANNELS // LANES))
Z_GROUPS = [[y * RING + z for z in range(RING)] for y in range(RING)]
Y_GROUPS = [[y * RING + z for y in range(RING)] for z in range(RING)]
X_GROUPS = [[x * 2 + core for x in range(XCHIPS)] for core in range(2)]
SIBLING = [(t, t ^ 1) for t in range(2 * XCHIPS)]


def over_subs(rows):
    return jnp.broadcast_to(rows[:, None, :], (POLES, SUBS, LANES))


def sub_index():
    return lax.broadcasted_iota(jnp.int32, (POLES, SUBS, LANES), 1).astype(jnp.float32)


def end_states(gate_ref, value_ref, rate_ref, x_ref, ends_ref, send_ref):
    product = gate_ref[...].astype(jnp.float32) * value_ref[...].astype(jnp.float32)
    product = product.astype(jnp.bfloat16).astype(jnp.float32)
    for g, lanes in enumerate(GROUPS):
        x_ref[g] = product[:, lanes]
        rate = rate_ref[:, lanes] / SEQ
        shrink = over_subs(jnp.exp(-rate))
        state = jnp.zeros((POLES, SUBS, LANES), jnp.float32)
        for t in range(STEPS):
            row = x_ref[g, pl.ds(t, SUBS, stride=STEPS), :]
            state = shrink * state + row[None]
        ends_ref[:, :, lanes] = state
        left = STEPS * (SUBS - 1.0 - sub_index())
        total = jnp.sum(state * jnp.exp(-over_subs(rate) * left), axis=1).astype(LINK)
        for j in range(RING):
            send_ref[j, :, lanes] = total


def chunk_carry(came_ref, rate_ref, prior_ref, send_ref):
    z = lax.rem(lax.axis_index("context"), RING)
    shrink = jnp.exp(-rate_ref[...] * (ROWS / SEQ))
    prior = jnp.zeros((POLES, CHANNELS), jnp.float32)
    total = jnp.zeros((POLES, CHANNELS), jnp.float32)
    for j in range(RING):
        came = came_ref[j].astype(jnp.float32)
        prior = jnp.where(j < z, prior * shrink + came, prior)
        total = total * shrink + came
    prior_ref[...] = prior
    sent = total.astype(LINK)
    for j in range(RING):
        send_ref[j] = sent


def convolve_project(
    came_ref, prior_ref, ends_ref, x_ref, query_ref, residue_ref, rate_ref, weight_ref,
    keep_ref, send_ref, y_ref,
):
    context = lax.axis_index("context")
    core = lax.rem(lax.axis_index("tensor"), 2)
    z, y = lax.rem(context, RING), context // RING
    shrink = jnp.exp(-rate_ref[...] * (RING * ROWS / SEQ))
    carry = jnp.zeros((POLES, CHANNELS), jnp.float32)
    for j in range(RING):
        carry = jnp.where(j < y, carry * shrink + came_ref[j].astype(jnp.float32), carry)
    behind = (z * ROWS).astype(jnp.float32) / SEQ
    carry = carry * jnp.exp(-rate_ref[...] * behind) + prior_ref[...]
    for g, lanes in enumerate(GROUPS):
        rate = rate_ref[:, lanes] / SEQ
        steps = over_subs(rate)
        shrink_sub = jnp.exp(-steps * STEPS)
        sub = sub_index()
        state = jnp.where(sub > 0, pltpu.roll(ends_ref[:, :, lanes], 1, 1), over_subs(carry[:, lanes]))
        for shift in (1, 2, 4):
            state = state + jnp.where(sub >= shift, pltpu.roll(state, shift, 1), 0.0) * shrink_sub
            shrink_sub = shrink_sub * shrink_sub
        shrink_one = over_subs(jnp.exp(-rate))
        residue = over_subs(residue_ref[:, lanes])
        for t in range(STEPS):
            row = x_ref[g, pl.ds(t, SUBS, stride=STEPS), :]
            state = shrink_one * state + row[None]
            y_ref[g, pl.ds(t, SUBS, stride=STEPS), :] = jnp.sum(residue * state, axis=0)
    convolved = jnp.concatenate([y_ref[g] for g in range(len(GROUPS))], axis=1)
    gated = (query_ref[...].astype(jnp.float32) * convolved).astype(jnp.bfloat16)
    for out_ref, owner in ((send_ref, 1 - core), (keep_ref, core)):
        for chip in range(XCHIPS):
            column = pl.multiple_of((2 * chip + owner) * CHANNELS, CHANNELS)
            partial = jnp.dot(
                gated, weight_ref[:, pl.ds(column, CHANNELS)], preferred_element_type=jnp.float32
            )
            out_ref[chip] = partial.astype(out_ref.dtype)


def add_pair(kept_ref, came_ref, out_ref):
    total = kept_ref[...].astype(jnp.float32) + came_ref[...].astype(jnp.float32)
    out_ref[...] = total.astype(out_ref.dtype)


def add_chips(came_ref, out_ref):
    total = came_ref[0].astype(jnp.float32)
    for chip in range(1, XCHIPS):
        total = total + came_ref[chip].astype(jnp.float32)
    out_ref[...] = total.astype(out_ref.dtype)


def kernel(body, outs, scratch=(), flops=0, moved=0):
    return pl.pallas_call(
        body,
        out_shape=[jax.ShapeDtypeStruct(shape, dtype) for shape, dtype in outs],
        scratch_shapes=scratch,
        compiler_params=pltpu.CompilerParams(vmem_limit_bytes=32 * 2**20),
        cost_estimate=pl.CostEstimate(flops=flops, bytes_accessed=moved, transcendentals=0),
    )


def on_device(queries, key_gate, values, residues, decay_rates, out_weight):
    f32, bf16 = jnp.float32, jnp.bfloat16
    block = (RING, POLES, CHANNELS)
    x, ends, sent = kernel(
        end_states,
        [((len(GROUPS), ROWS, LANES), f32), ((POLES, SUBS, CHANNELS), f32), (block, LINK)],
        flops=8_000_000, moved=1_000_000,
    )(key_gate, values, decay_rates)
    came = lax.all_to_all(sent, "context", 0, 0, axis_index_groups=Z_GROUPS)
    prior, sent = kernel(
        chunk_carry, [((POLES, CHANNELS), f32), (block, LINK)], flops=500_000, moved=300_000
    )(came, decay_rates)
    came = lax.all_to_all(sent, "context", 0, 0, axis_index_groups=Y_GROUPS)
    halves = (XCHIPS, ROWS, CHANNELS)
    kept, sent = kernel(
        convolve_project,
        [(halves, bf16), (halves, bf16)],
        scratch=[pltpu.VMEM((len(GROUPS), ROWS, LANES), f32)],
        flops=600_000_000, moved=6_000_000,
    )(came, prior, ends, x, queries, residues, decay_rates, out_weight)
    came = lax.ppermute(sent, "tensor", SIBLING)
    (pair,) = kernel(add_pair, [(halves, bf16)], flops=300_000, moved=1_500_000)(kept, came)
    came = lax.all_to_all(pair, "tensor", 0, 0, axis_index_groups=X_GROUPS)
    (mixed,) = kernel(add_chips, [((ROWS, CHANNELS), bf16)], flops=300_000, moved=700_000)(came)
    return mixed


def solution(mesh):
    in_specs = (
        P("context", "tensor"),
        P("context", "tensor"),
        P("context", "tensor"),
        P(None, "tensor"),
        P(None, "tensor"),
        P("tensor", None),
    )
    out_specs = P("context", "tensor")
    return jax.shard_map(
        on_device, mesh=mesh, in_specs=in_specs, out_specs=out_specs, check_vma=False
    )
```

time: 207 us -> 63.4 us (0.31)
  waiting for transfers between devices: 84.7 us -> 1.51 us
  starting transfers between devices: 23.8 us -> 5.53 us
  matrix products: 16.3 us -> 0 us
  between operations: 15.3 us -> 0.04 us
  other arithmetic: 11.2 us -> 0 us
  local copies, waits for them, and re-layouts: 11.8 us -> 7.17 us
  Pallas kernels: 0 us -> 3.11 us
  blocking collectives: 42.6 us -> 45.5 us
    psum x1 -> x0, waiting for transfers between devices: 65.4 us -> none  [on_device(): lax.psum(partial_value.astype(jnp.bfloat16), 'tensor').astype(jnp.float32)]
    all_to_all x2 -> x0, starting transfers between devices: 23.6 us -> none  [the longest x1 17.1 us: spectral_conv(): lax.all_to_all(signal.reshape(1, row_count, channels), 'context', split_a...]
    all_to_all x2 -> x0, waiting for transfers between devices: 19.3 us -> none  [the longest x1 13.6 us: spectral_conv(): lax.all_to_all(packed.astype(jnp.bfloat16), 'context', split_axis=0, conc...]
    dot_general x17 -> x0, matrix products: 16.3 us -> none  [the longest x16 12.4 us: matmul(): jnp.dot(left, right, precision=table_prec, preferred_element_type=jnp.flo...]
    ppermute x0 -> x1, starting transfers between devices: none -> 5.53 us  [on_device(): came = lax.ppermute(sent, 'tensor', SIBLING)]
    unnamed x169 -> x14, local copies, waits for them, and re-layouts: 2.04 us -> 7.17 us
    reshape x9 -> x0, local copies, waits for them, and re-layouts: 3.75 us -> none  [the longest x2 0.88 us: spectral_conv(): real_part = real_part.reshape(block_count, piece_rows, 2, channels)]
    exp x3 -> x0, other arithmetic: 3.19 us -> none  [filter_spectrum(): jnp.exp(-decay_rates[pole_index])]
  transfers between devices with their start and end apart: 3 -> 1, of which waited for: 3 -> 1; matrix products, arithmetic and copies ran while one was open for 3% -> 0% of each run, Pallas kernels for 0% -> 0%
where the time goes in v1:
time: 63.4 us; the launch traced here: 62.9 us
  blocking collectives  45.5 us (72%)
  local copies, waits for them, and re-layouts  7.17 us (11%)
  starting transfers between devices  5.53 us (9%)
  Pallas kernels  3.11 us (5%)
  waiting for transfers between devices  1.51 us (2%)
    all_to_all x1, blocking collectives, on_device(): came = lax.all_to_all(sent, 'context', 0, 0, axis_index_groups=Z_GROUPS)  18.4 us
    all_to_all x1, blocking collectives, on_device(): came = lax.all_to_all(sent, 'context', 0, 0, axis_index_groups=Y_GROUPS)  14.6 us
    all_to_all x1, blocking collectives, on_device(): came = lax.all_to_all(pair, 'tensor', 0, 0, axis_index_groups=X_GROUPS)  12.4 us
    unnamed x14, local copies, waits for them, and re-layouts  7.17 us
    ppermute x1, starting transfers between devices, on_device(): came = lax.ppermute(sent, 'tensor', SIBLING)  5.53 us
    pallas_call x1, Pallas kernels, on_device(): kernel(convolve_project, [(halves, bf16), (halves, bf16)], scratch=[pltpu...  1.63 us
    ppermute x1, waiting for transfers between devices, on_device(): came = lax.ppermute(sent, 'tensor', SIBLING)  1.51 us
  transfers between devices with their start and end apart: 1, of which 1 were waited for; matrix products, arithmetic and copies ran while one was open for 0% of the time, Pallas kernels for 0%

profile of v1, /device:TPU:1, one launch (start us, length us, event | category | flops | bytes accessed | tf_op | source)
XLA Modules:
  0.0 62.9 jit_solution(635884520226684911)
XLA Ops:
  0.0 0.0 copy-start.1
  0.0 0.8 %copy-done.1 = f32[16,512]{1,0:T(8,128)S(1)} copy-done((f32[16,512]{1,0:T(8,128)S(1)}, f32[16,512]{1,0:T(8,128)}, u32[]{:S(2)}) %copy-start.1) | copy-done | bytes 32792
  0.8 0.0 copy-start.4
  0.8 0.9 %copy-done.4 = bf16[128,512]{1,0:T(8,128)(2,1)S(1)} copy-done((bf16[128,512]{1,0:T(8,128)(2,1)S(1)}, bf16[128,512]{1,0:T(8,128)(2,1)}, u32[]{:S(2)}) %copy-start.4) | copy-done | bytes 131096
  1.7 0.0 copy-start.5
  1.7 0.9 %copy-done.5 = bf16[128,512]{1,0:T(8,128)(2,1)S(1)} copy-done((bf16[128,512]{1,0:T(8,128)(2,1)S(1)}, bf16[128,512]{1,0:T(8,128)(2,1)}, u32[]{:S(2)}) %copy-start.5) | copy-done | bytes 131096
  2.6 0.6 shard_map.64
  3.1 18.4 %all_to_all.15.came_ref = bf16[8,16,512]{2,1,0:T(8,128)(2,1)S(1)} all-to-all(bf16[8,16,512]{2,1,0:T(8,128)(2,1)S(1)} %get-tuple-element.12), channel_id=1, replica_groups={{0,8,16,24,32,40,48,56},{64,72,80,88,96,104,112,120},{128,136,144,152,1..., dimensions={0} | all-to-all | bytes 262144 | tf_op jit(solution)/shard_map/all_to_all | solution.py:136
  21.6 0.0 copy-start.2
  21.6 0.8 %copy-done.2 = f32[16,512]{1,0:T(8,128)S(1)} copy-done((f32[16,512]{1,0:T(8,128)S(1)}, f32[16,512]{1,0:T(8,128)}, u32[]{:S(2)}) %copy-start.2) | copy-done | bytes 32792
  22.3 0.1 shard_map.65
  22.4 14.6 %all_to_all.16.came_ref = bf16[8,16,512]{2,1,0:T(8,128)(2,1)S(1)} all-to-all(bf16[8,16,512]{2,1,0:T(8,128)(2,1)S(1)} %get-tuple-element.13), channel_id=1, replica_groups={{0,64,128,192,256,320,384,448},{8,72,136,200,264,328,392,456},{16,80,14..., dimensions={0} | all-to-all | bytes 262144 | tf_op jit(solution)/shard_map/all_to_all | solution.py:140
  37.1 0.0 copy-start
  37.1 2.2 %copy-done = bf16[512,4096]{1,0:T(8,128)(2,1)S(1)} copy-done((bf16[512,4096]{1,0:T(8,128)(2,1)S(1)}, bf16[512,4096]{1,0:T(8,128)(2,1)}, u32[]{:S(2)}) %copy-start) | copy-done | bytes 4194328
  39.2 0.0 copy-start.3
  39.2 0.9 %copy-done.3 = bf16[128,512]{1,0:T(8,128)(2,1)S(1)} copy-done((bf16[128,512]{1,0:T(8,128)(2,1)S(1)}, bf16[128,512]{1,0:T(8,128)(2,1)}, u32[]{:S(2)}) %copy-start.3) | copy-done | bytes 131096
  40.1 0.0 copy-start.6
  40.1 0.8 %copy-done.6 = f32[16,512]{1,0:T(8,128)S(1)} copy-done((f32[16,512]{1,0:T(8,128)S(1)}, f32[16,512]{1,0:T(8,128)}, u32[]{:S(2)}) %copy-start.6) | copy-done | bytes 32792
  40.9 1.6 %shard_map.66 = (bf16[4,128,512]{2,1,0:T(8,128)(2,1)S(1)}, bf16[4,128,512]{2,1,0:T(8,128)(2,1)S(1)}) custom-call(bf16[8,16,512]{2,1,0:T(8,128)(2,1)S(1)} %all_to_all.16.came_ref, f32[16,512]{1,0:T(8,128)S(1)} %get-tuple-element.14.prior_ref, f32[16,8,512]{2,1,0:T(8,128)S(1)} %get-tuple-element.15.ends_ref, f32[4,128,128]{2,1,0:T(8,128)S(1)} %get-tuple-element.16.x_ref, ...), custom_call_target="tpu_custom_call" | custom-call | flops 600000000 | bytes 6000000 | tf_op jit(solution)/shard_map/pallas_call | solution.py:142
  42.5 5.5 %collective-permute-start = (bf16[4,128,512]{2,1,0:T(8,128)(2,1)S(1)}, bf16[4,128,512]{2,1,0:T(8,128)(2,1)S(1)}, u32[]{:S(2)}, u32[]{:S(2)}) collective-permute-start(bf16[4,128,512]{2,1,0:T(8,128)(2,1)S(1)} %get-tuple-element.18), channel_id=1, source_target_pairs={{0,1},{1,0},{2,3},{3,2},{4,5},{5,4},{6,7},{7,6},{8,9},{9,8},{10,11... | collective-permute-start | bytes 1572872 | tf_op jit(solution)/shard_map/ppermute | solution.py:148
  48.1 1.5 %collective-permute-done.came_ref = bf16[4,128,512]{2,1,0:T(8,128)(2,1)S(1)} collective-permute-done((bf16[4,128,512]{2,1,0:T(8,128)(2,1)S(1)}, bf16[4,128,512]{2,1,0:T(8,128)(2,1)S(1)}, u32[]{:S(2)}, u32[]{:S(2)}) %collective-permute-start) | collective-permute-done | bytes 524320 | tf_op jit(solution)/shard_map/ppermute | solution.py:148
  49.6 0.1 shard_map.67
  49.7 12.4 %all_to_all.17.came_ref = bf16[4,128,512]{2,1,0:T(8,128)(2,1)S(1)} all-to-all(bf16[4,128,512]{2,1,0:T(8,128)(2,1)S(1)} %shard_map.67), channel_id=1, replica_groups={{0,2,4,6},{1,3,5,7},{8,10,12,14},{9,11,13,15},{16,18,20,22},{17,19,21,2..., dimensions={0} | all-to-all | bytes 1048576 | tf_op jit(solution)/shard_map/all_to_all | solution.py:150
  62.1 0.7 %shard_map.68 = bf16[128,512]{1,0:T(8,128)(2,1)} custom-call(bf16[4,128,512]{2,1,0:T(8,128)(2,1)S(1)} %all_to_all.17.came_ref), custom_call_target="tpu_custom_call" | custom-call | flops 300000 | bytes 700000 | tf_op jit(solution)/shard_map/pallas_call | solution.py:151
Async XLA Ops:
  0.0 0.8 %copy-start.1 = (f32[16,512]{1,0:T(8,128)S(1)}, f32[16,512]{1,0:T(8,128)}, u32[]{:S(2)}) copy-start(f32[16,512]{1,0:T(8,128)} %rate_ref.5) | copy-start | bytes 98308
  0.8 0.9 %copy-start.4 = (bf16[128,512]{1,0:T(8,128)(2,1)S(1)}, bf16[128,512]{1,0:T(8,128)(2,1)}, u32[]{:S(2)}) copy-start(bf16[128,512]{1,0:T(8,128)(2,1)} %gate_ref.1) | copy-start | bytes 393220
  1.7 0.9 %copy-start.5 = (bf16[128,512]{1,0:T(8,128)(2,1)S(1)}, bf16[128,512]{1,0:T(8,128)(2,1)}, u32[]{:S(2)}) copy-start(bf16[128,512]{1,0:T(8,128)(2,1)} %value_ref.1) | copy-start | bytes 393220
  21.6 0.8 %copy-start.2 = (f32[16,512]{1,0:T(8,128)S(1)}, f32[16,512]{1,0:T(8,128)}, u32[]{:S(2)}) copy-start(f32[16,512]{1,0:T(8,128)} %rate_ref.5) | copy-start | bytes 98308
  37.1 2.2 %copy-start = (bf16[512,4096]{1,0:T(8,128)(2,1)S(1)}, bf16[512,4096]{1,0:T(8,128)(2,1)}, u32[]{:S(2)}) copy-start(bf16[512,4096]{1,0:T(8,128)(2,1)} %weight_ref.1) | copy-start | bytes 12582916
  39.2 0.9 %copy-start.3 = (bf16[128,512]{1,0:T(8,128)(2,1)S(1)}, bf16[128,512]{1,0:T(8,128)(2,1)}, u32[]{:S(2)}) copy-start(bf16[128,512]{1,0:T(8,128)(2,1)} %query_ref.1) | copy-start | bytes 393220
  40.1 0.8 %copy-start.6 = (f32[16,512]{1,0:T(8,128)S(1)}, f32[16,512]{1,0:T(8,128)}, u32[]{:S(2)}) copy-start(f32[16,512]{1,0:T(8,128)} %residue_ref.1) | copy-start | bytes 98308
  42.5 7.1 %collective-permute-start = (bf16[4,128,512]{2,1,0:T(8,128)(2,1)S(1)}, bf16[4,128,512]{2,1,0:T(8,128)(2,1)S(1)}, u32[]{:S(2)}, u32[]{:S(2)}) collective-permute-start(bf16[4,128,512]{2,1,0:T(8,128)(2,1)S(1)} %get-tuple-element.18), channel_id=1, source_target_pairs={{0,1},{1,0},{2,3},{3,2},{4,5},{5,4},{6,7},{7,6},{8,9},{9,8},{10,11... | collective-permute-start | bytes 1572872 | tf_op jit(solution)/shard_map/ppermute | solution.py:148

commit v2 on v1

--- a/solution.py
+++ b/solution.py
@@ -31,7 +31,15 @@
     return lax.broadcasted_iota(jnp.int32, (POLES, SUBS, LANES), 1).astype(jnp.float32)
 
 
-def end_states(gate_ref, value_ref, rate_ref, x_ref, ends_ref, send_ref):
+def end_states(
+    gate_hbm, value_hbm, rate_hbm, x_ref, ends_ref, send_ref, gate_ref, value_ref, rate_ref, sems
+):
+    pairs = ((gate_hbm, gate_ref), (value_hbm, value_ref), (rate_hbm, rate_ref))
+    copies = [pltpu.make_async_copy(a, b, sems.at[i]) for i, (a, b) in enumerate(pairs)]
+    for copy in copies:
+        copy.start()
+    for copy in copies:
+        copy.wait()
     product = gate_ref[...].astype(jnp.float32) * value_ref[...].astype(jnp.float32)
     product = product.astype(jnp.bfloat16).astype(jnp.float32)
     for g, lanes in enumerate(GROUPS):
@@ -66,7 +74,7 @@
 
 def convolve_project(
     came_ref, prior_ref, ends_ref, x_ref, query_ref, residue_ref, rate_ref, weight_ref,
-    keep_ref, send_ref, y_ref,
+    send_ref, gated_ref, y_ref,
 ):
     context = lax.axis_index("context")
     core = lax.rem(lax.axis_index("tensor"), 2)
@@ -94,13 +102,21 @@
             y_ref[g, pl.ds(t, SUBS, stride=STEPS), :] = jnp.sum(residue * state, axis=0)
     convolved = jnp.concatenate([y_ref[g] for g in range(len(GROUPS))], axis=1)
     gated = (query_ref[...].astype(jnp.float32) * convolved).astype(jnp.bfloat16)
-    for out_ref, owner in ((send_ref, 1 - core), (keep_ref, core)):
-        for chip in range(XCHIPS):
-            column = pl.multiple_of((2 * chip + owner) * CHANNELS, CHANNELS)
-            partial = jnp.dot(
-                gated, weight_ref[:, pl.ds(column, CHANNELS)], preferred_element_type=jnp.float32
-            )
-            out_ref[chip] = partial.astype(out_ref.dtype)
+    gated_ref[...] = gated
+    project(gated, weight_ref, 1 - core, send_ref)
+
+
+def project(gated, weight_ref, core, out_ref):
+    for chip in range(XCHIPS):
+        column = pl.multiple_of((2 * chip + core) * CHANNELS, CHANNELS)
+        partial = jnp.dot(
+            gated, weight_ref[:, pl.ds(column, CHANNELS)], preferred_element_type=jnp.float32
+        )
+        out_ref[chip] = partial.astype(out_ref.dtype)
+
+
+def project_own(gated_ref, weight_ref, keep_ref):
+    project(gated_ref[...], weight_ref, lax.rem(lax.axis_index("tensor"), 2), keep_ref)
 
 
 def add_pair(kept_ref, came_ref, out_ref):
@@ -115,9 +131,10 @@
     out_ref[...] = total.astype(out_ref.dtype)
 
 
-def kernel(body, outs, scratch=(), flops=0, moved=0):
+def kernel(body, outs, scratch=(), flops=0, moved=0, **specs):
     return pl.pallas_call(
         body,
+        **specs,
         out_shape=[jax.ShapeDtypeStruct(shape, dtype) for shape, dtype in outs],
         scratch_shapes=scratch,
         compiler_params=pltpu.CompilerParams(vmem_limit_bytes=32 * 2**20),
@@ -128,27 +145,38 @@
 def on_device(queries, key_gate, values, residues, decay_rates, out_weight):
     f32, bf16 = jnp.float32, jnp.bfloat16
     block = (RING, POLES, CHANNELS)
+    rows, modes = (ROWS, CHANNELS), (POLES, CHANNELS)
     x, ends, sent = kernel(
         end_states,
         [((len(GROUPS), ROWS, LANES), f32), ((POLES, SUBS, CHANNELS), f32), (block, LINK)],
-        flops=8_000_000, moved=1_000_000,
-    )(key_gate, values, decay_rates)
+        scratch=[
+            pltpu.VMEM(rows, bf16),
+            pltpu.VMEM(rows, bf16),
+            pltpu.VMEM(modes, f32),
+            pltpu.SemaphoreType.DMA((3,)),
+        ],
+        in_specs=[pl.BlockSpec(memory_space=pltpu.HBM)] * 3,
+        flops=8_000_000_000, moved=1_000_000,
+    )(*(pltpu.with_memory_space_constraint(a, pltpu.HBM) for a in (key_gate, values, decay_rates)))
     came = lax.all_to_all(sent, "context", 0, 0, axis_index_groups=Z_GROUPS)
     prior, sent = kernel(
-        chunk_carry, [((POLES, CHANNELS), f32), (block, LINK)], flops=500_000, moved=300_000
+        chunk_carry, [(modes, f32), (block, LINK)], flops=8_000_000_000, moved=300_000
     )(came, decay_rates)
     came = lax.all_to_all(sent, "context", 0, 0, axis_index_groups=Y_GROUPS)
     halves = (XCHIPS, ROWS, CHANNELS)
-    kept, sent = kernel(
+    sent, gated = kernel(
         convolve_project,
-        [(halves, bf16), (halves, bf16)],
+        [(halves, bf16), (rows, bf16)],
         scratch=[pltpu.VMEM((len(GROUPS), ROWS, LANES), f32)],
-        flops=600_000_000, moved=6_000_000,
+        flops=300_000_000, moved=3_000_000,
     )(came, prior, ends, x, queries, residues, decay_rates, out_weight)
     came = lax.ppermute(sent, "tensor", SIBLING)
+    (kept,) = kernel(project_own, [(halves, f32)], flops=600_000_000, moved=3_000_000)(
+        gated, out_weight
+    )
     (pair,) = kernel(add_pair, [(halves, bf16)], flops=300_000, moved=1_500_000)(kept, came)
     came = lax.all_to_all(pair, "tensor", 0, 0, axis_index_groups=X_GROUPS)
-    (mixed,) = kernel(add_chips, [((ROWS, CHANNELS), bf16)], flops=300_000, moved=700_000)(came)
+    (mixed,) = kernel(add_chips, [(rows, bf16)], flops=300_000, moved=700_000)(came)
     return mixed
 
 

time: 63.4 us -> 56.9 us (0.90)
  local copies, waits for them, and re-layouts: 7.17 us -> 0.01 us
  Pallas kernels: 3.11 us -> 4.27 us
    unnamed x14 -> x8, local copies, waits for them, and re-layouts: 7.17 us -> 0.01 us
    pallas_call x1, Pallas kernels: 0.56 us -> 1.57 us  [on_device(): kernel(end_states, [((len(GROUPS), ROWS, LANES), f32), ((POLES, SUBS, CHA...]
    pallas_call x3 -> x4, Pallas kernels: 2.42 us -> 2.62 us  [the longest x1 1.37 us: on_device(): kernel(convolve_project, [(halves, bf16), (rows, bf16)], scratch=[pltpu.V...]
  transfers between devices with their start and end apart: 1 -> 1, of which waited for: 1 -> 1; matrix products, arithmetic and copies ran while one was open for 0% -> 0% of each run, Pallas kernels for 0% -> 1%
where the time goes in v2:
time: 56.9 us; the launch traced here: 56.7 us
  blocking collectives  45.8 us (80%)
  starting transfers between devices  5.54 us (10%)
  Pallas kernels  4.27 us (8%)
  waiting for transfers between devices  1.05 us (2%)
    all_to_all x1, blocking collectives, on_device(): came = lax.all_to_all(sent, 'context', 0, 0, axis_index_groups=Z_GROUPS)  18.4 us
    all_to_all x1, blocking collectives, on_device(): came = lax.all_to_all(sent, 'context', 0, 0, axis_index_groups=Y_GROUPS)  14.9 us
    all_to_all x1, blocking collectives, on_device(): came = lax.all_to_all(pair, 'tensor', 0, 0, axis_index_groups=X_GROUPS)  12.4 us
    ppermute x1, starting transfers between devices, on_device(): came = lax.ppermute(sent, 'tensor', SIBLING)  5.54 us
    pallas_call x1, Pallas kernels, on_device(): kernel(end_states, [((len(GROUPS), ROWS, LANES), f32), ((POLES, SUBS, CHA...  1.57 us
    pallas_call x1, Pallas kernels, on_device(): kernel(convolve_project, [(halves, bf16), (rows, bf16)], scratch=[pltpu.V...  1.37 us
  transfers between devices with their start and end apart: 1, of which 1 were waited for; matrix products, arithmetic and copies ran while one was open for 0% of the time, Pallas kernels for 1%

profile of v2, /device:TPU:1, one launch (start us, length us, event | category | flops | bytes accessed | tf_op | source)
XLA Modules:
  0.0 56.7 jit_solution(10465149489284618895)
XLA Ops:
  0.0 0.0 copy-start.2
  0.0 1.6 %shard_map.64 = (f32[4,128,128]{2,1,0:T(8,128)S(1)}, f32[16,8,512]{2,1,0:T(8,128)S(1)}, bf16[8,16,512]{2,1,0:T(8,128)(2,1)S(1)}) custom-call(bf16[128,512]{1,0:T(8,128)(2,1)} %gate_hbm.1, bf16[128,512]{1,0:T(8,128)(2,1)} %value_hbm.1, f32[16,512]{1,0:T(8,128)} %rate_ref.3), custom_call_target="tpu_custom_call" | custom-call | flops 8000000000 | bytes 1000000 | tf_op jit(solution)/shard_map/pallas_call | solution.py:149
  1.6 18.4 %all_to_all.15.came_ref = bf16[8,16,512]{2,1,0:T(8,128)(2,1)S(1)} all-to-all(bf16[8,16,512]{2,1,0:T(8,128)(2,1)S(1)} %get-tuple-element.12), channel_id=1, replica_groups={{0,8,16,24,32,40,48,56},{64,72,80,88,96,104,112,120},{128,136,144,152,1..., dimensions={0} | all-to-all | bytes 262144 | tf_op jit(solution)/shard_map/all_to_all | solution.py:161
  20.0 0.0 copy-done.2
  20.0 0.0 copy-start
  20.0 0.0 copy-start.1
  20.0 0.0 copy-start.3
  20.0 0.1 shard_map.65
  20.1 14.9 %all_to_all.16.came_ref = bf16[8,16,512]{2,1,0:T(8,128)(2,1)S(1)} all-to-all(bf16[8,16,512]{2,1,0:T(8,128)(2,1)S(1)} %get-tuple-element.13), channel_id=1, replica_groups={{0,64,128,192,256,320,384,448},{8,72,136,200,264,328,392,456},{16,80,14..., dimensions={0} | all-to-all | bytes 262144 | tf_op jit(solution)/shard_map/all_to_all | solution.py:165
  35.0 0.0 copy-done
  35.0 0.0 copy-done.1
  35.0 0.0 copy-done.3
  35.0 1.4 %shard_map.66 = (bf16[4,128,512]{2,1,0:T(8,128)(2,1)S(1)}, bf16[128,512]{1,0:T(8,128)(2,1)S(1)}) custom-call(bf16[8,16,512]{2,1,0:T(8,128)(2,1)S(1)} %all_to_all.16.came_ref, f32[16,512]{1,0:T(8,128)S(1)} %get-tuple-element.14.prior_ref, f32[16,8,512]{2,1,0:T(8,128)S(1)} %get-tuple-element.15.ends_ref, f32[4,128,128]{2,1,0:T(8,128)S(1)} %get-tuple-element.16.x_ref, ...), custom_call_target="tpu_custom_call" | custom-call | flops 300000000 | bytes 3000000 | tf_op jit(solution)/shard_map/pallas_call | solution.py:167
  36.4 5.5 %collective-permute-start = (bf16[4,128,512]{2,1,0:T(8,128)(2,1)S(1)}, bf16[4,128,512]{2,1,0:T(8,128)(2,1)S(1)}, u32[]{:S(2)}, u32[]{:S(2)}) collective-permute-start(bf16[4,128,512]{2,1,0:T(8,128)(2,1)S(1)} %get-tuple-element.18), channel_id=1, source_target_pairs={{0,1},{1,0},{2,3},{3,2},{4,5},{5,4},{6,7},{7,6},{8,9},{9,8},{10,11... | collective-permute-start | bytes 1572872 | tf_op jit(solution)/shard_map/ppermute | solution.py:173
  41.9 0.5 shard_map.67.kept_ref
  42.4 1.0 %collective-permute-done.came_ref = bf16[4,128,512]{2,1,0:T(8,128)(2,1)S(1)} collective-permute-done((bf16[4,128,512]{2,1,0:T(8,128)(2,1)S(1)}, bf16[4,128,512]{2,1,0:T(8,128)(2,1)S(1)}, u32[]{:S(2)}, u32[]{:S(2)}) %collective-permute-start) | collective-permute-done | bytes 524320 | tf_op jit(solution)/shard_map/ppermute | solution.py:173
  43.5 0.1 shard_map.68
  43.6 12.4 %all_to_all.17.came_ref = bf16[4,128,512]{2,1,0:T(8,128)(2,1)S(1)} all-to-all(bf16[4,128,512]{2,1,0:T(8,128)(2,1)S(1)} %shard_map.68), channel_id=1, replica_groups={{0,2,4,6},{1,3,5,7},{8,10,12,14},{9,11,13,15},{16,18,20,22},{17,19,21,2..., dimensions={0} | all-to-all | bytes 1048576 | tf_op jit(solution)/shard_map/all_to_all | solution.py:178
  56.0 0.7 %shard_map.69 = bf16[128,512]{1,0:T(8,128)(2,1)} custom-call(bf16[4,128,512]{2,1,0:T(8,128)(2,1)S(1)} %all_to_all.17.came_ref), custom_call_target="tpu_custom_call" | custom-call | flops 300000 | bytes 700000 | tf_op jit(solution)/shard_map/pallas_call | solution.py:179
Async XLA Ops:
  0.0 20.0 %copy-start.2 = (f32[16,512]{1,0:T(8,128)S(1)}, f32[16,512]{1,0:T(8,128)}, u32[]{:S(2)}) copy-start(f32[16,512]{1,0:T(8,128)} %rate_ref.3) | copy-start | bytes 98308
  20.0 15.0 %copy-start = (bf16[512,4096]{1,0:T(8,128)(2,1)S(1)}, bf16[512,4096]{1,0:T(8,128)(2,1)}, u32[]{:S(2)}) copy-start(bf16[512,4096]{1,0:T(8,128)(2,1)} %weight_ref.3) | copy-start | bytes 12582916
  20.0 15.0 %copy-start.1 = (bf16[128,512]{1,0:T(8,128)(2,1)S(1)}, bf16[128,512]{1,0:T(8,128)(2,1)}, u32[]{:S(2)}) copy-start(bf16[128,512]{1,0:T(8,128)(2,1)} %query_ref.1) | copy-start | bytes 393220
  20.0 15.0 %copy-start.3 = (f32[16,512]{1,0:T(8,128)S(1)}, f32[16,512]{1,0:T(8,128)}, u32[]{:S(2)}) copy-start(f32[16,512]{1,0:T(8,128)} %residue_ref.1) | copy-start | bytes 98308
  36.4 7.1 %collective-permute-start = (bf16[4,128,512]{2,1,0:T(8,128)(2,1)S(1)}, bf16[4,128,512]{2,1,0:T(8,128)(2,1)S(1)}, u32[]{:S(2)}, u32[]{:S(2)}) collective-permute-start(bf16[4,128,512]{2,1,0:T(8,128)(2,1)S(1)} %get-tuple-element.18), channel_id=1, source_target_pairs={{0,1},{1,0},{2,3},{3,2},{4,5},{5,4},{6,7},{7,6},{8,9},{9,8},{10,11... | collective-permute-start | bytes 1572872 | tf_op jit(solution)/shard_map/ppermute | solution.py:173

commit v3 on v2

--- a/solution.py
+++ b/solution.py
@@ -13,14 +13,17 @@
 SUBS = 8
 STEPS = ROWS // SUBS
 RING = 8
-XCHIPS = 4
 LINK = jnp.bfloat16
 
 GROUPS = tuple(slice(g * LANES, (g + 1) * LANES) for g in range(CHANNELS // LANES))
 Z_GROUPS = [[y * RING + z for z in range(RING)] for y in range(RING)]
 Y_GROUPS = [[y * RING + z for y in range(RING)] for z in range(RING)]
-X_GROUPS = [[x * 2 + core for x in range(XCHIPS)] for core in range(2)]
-SIBLING = [(t, t ^ 1) for t in range(2 * XCHIPS)]
+TENSOR = 8
+DOWN = [(t, (t - 1) % TENSOR) for t in range(TENSOR)]
+UP = [(t, (t + 1) % TENSOR) for t in range(TENSOR)]
+DOWN_BLOCKS = (-4, -3, -2, -1)
+UP_BLOCKS = (3, 2, 1)
+LATER_BLOCKS = (-3, 2, -2, 1, -1, 0)
 
 
 def over_subs(rows):
@@ -74,10 +77,9 @@
 
 def convolve_project(
     came_ref, prior_ref, ends_ref, x_ref, query_ref, residue_ref, rate_ref, weight_ref,
-    send_ref, gated_ref, y_ref,
+    down_ref, up_ref, gated_ref, y_ref,
 ):
     context = lax.axis_index("context")
-    core = lax.rem(lax.axis_index("tensor"), 2)
     z, y = lax.rem(context, RING), context // RING
     shrink = jnp.exp(-rate_ref[...] * (RING * ROWS / SEQ))
     carry = jnp.zeros((POLES, CHANNELS), jnp.float32)
@@ -103,31 +105,30 @@
     convolved = jnp.concatenate([y_ref[g] for g in range(len(GROUPS))], axis=1)
     gated = (query_ref[...].astype(jnp.float32) * convolved).astype(jnp.bfloat16)
     gated_ref[...] = gated
-    project(gated, weight_ref, 1 - core, send_ref)
-
-
-def project(gated, weight_ref, core, out_ref):
-    for chip in range(XCHIPS):
-        column = pl.multiple_of((2 * chip + core) * CHANNELS, CHANNELS)
-        partial = jnp.dot(
-            gated, weight_ref[:, pl.ds(column, CHANNELS)], preferred_element_type=jnp.float32
-        )
-        out_ref[chip] = partial.astype(out_ref.dtype)
-
-
-def project_own(gated_ref, weight_ref, keep_ref):
-    project(gated_ref[...], weight_ref, lax.rem(lax.axis_index("tensor"), 2), keep_ref)
-
-
-def add_pair(kept_ref, came_ref, out_ref):
-    total = kept_ref[...].astype(jnp.float32) + came_ref[...].astype(jnp.float32)
-    out_ref[...] = total.astype(out_ref.dtype)
-
-
-def add_chips(came_ref, out_ref):
-    total = came_ref[0].astype(jnp.float32)
-    for chip in range(1, XCHIPS):
-        total = total + came_ref[chip].astype(jnp.float32)
+    down_ref[...] = project(gated, weight_ref, DOWN_BLOCKS[0]).astype(LINK)
+    up_ref[...] = project(gated, weight_ref, UP_BLOCKS[0]).astype(LINK)
+
+
+def project(gated, weight_ref, offset):
+    owner = lax.rem(lax.axis_index("tensor") + (offset + TENSOR), TENSOR)
+    column = pl.multiple_of(owner * CHANNELS, CHANNELS)
+    return jnp.dot(
+        gated, weight_ref[:, pl.ds(column, CHANNELS)], preferred_element_type=jnp.float32
+    )
+
+
+def project_later(gated_ref, weight_ref, *out_refs):
+    gated = gated_ref[...]
+    for offset, out_ref in zip(LATER_BLOCKS, out_refs):
+        out_ref[...] = project(gated, weight_ref, offset)
+
+
+def add_own(came_ref, own_ref, out_ref):
+    out_ref[...] = (came_ref[...].astype(jnp.float32) + own_ref[...]).astype(out_ref.dtype)
+
+
+def add_both(down_ref, up_ref, own_ref, out_ref):
+    total = down_ref[...].astype(jnp.float32) + up_ref[...].astype(jnp.float32) + own_ref[...]
     out_ref[...] = total.astype(out_ref.dtype)
 
 
@@ -163,20 +164,24 @@
         chunk_carry, [(modes, f32), (block, LINK)], flops=8_000_000_000, moved=300_000
     )(came, decay_rates)
     came = lax.all_to_all(sent, "context", 0, 0, axis_index_groups=Y_GROUPS)
-    halves = (XCHIPS, ROWS, CHANNELS)
-    sent, gated = kernel(
+    down, up, gated = kernel(
         convolve_project,
-        [(halves, bf16), (rows, bf16)],
+        [(rows, LINK), (rows, LINK), (rows, bf16)],
         scratch=[pltpu.VMEM((len(GROUPS), ROWS, LANES), f32)],
         flops=300_000_000, moved=3_000_000,
     )(came, prior, ends, x, queries, residues, decay_rates, out_weight)
-    came = lax.ppermute(sent, "tensor", SIBLING)
-    (kept,) = kernel(project_own, [(halves, f32)], flops=600_000_000, moved=3_000_000)(
-        gated, out_weight
-    )
-    (pair,) = kernel(add_pair, [(halves, bf16)], flops=300_000, moved=1_500_000)(kept, came)
-    came = lax.all_to_all(pair, "tensor", 0, 0, axis_index_groups=X_GROUPS)
-    (mixed,) = kernel(add_chips, [(rows, bf16)], flops=300_000, moved=700_000)(came)
+    down = lax.ppermute(down, "tensor", DOWN)
+    up = lax.ppermute(up, "tensor", UP)
+    own = kernel(
+        project_later, [(rows, f32)] * len(LATER_BLOCKS), flops=400_000_000, moved=3_000_000
+    )(gated, out_weight)
+    own = dict(zip(LATER_BLOCKS, own))
+    add = kernel(add_own, [(rows, LINK)], flops=100_000, moved=500_000)
+    for block in DOWN_BLOCKS[1:]:
+        down = lax.ppermute(add(down, own[block])[0], "tensor", DOWN)
+    for block in UP_BLOCKS[1:]:
+        up = lax.ppermute(add(up, own[block])[0], "tensor", UP)
+    (mixed,) = kernel(add_both, [(rows, bf16)], flops=200_000, moved=600_000)(down, up, own[0])
     return mixed
 
 

time: 56.9 us -> 59.6 us (1.047)
  the two profiles are of different devices: /device:TPU:1 before, /device:TPU:7 now
where the time goes in v3:
time: 59.6 us; the launch traced here: 59.4 us
  blocking collectives  32.5 us (55%)
  waiting for transfers between devices  12.8 us (21%)
  starting transfers between devices  9.66 us (16%)
  Pallas kernels  4.26 us (7%)
    all_to_all x1, blocking collectives, on_device(): came = lax.all_to_all(sent, 'context', 0, 0, axis_index_groups=Z_GROUPS)  17.6 us
    all_to_all x1, blocking collectives, on_device(): came = lax.all_to_all(sent, 'context', 0, 0, axis_index_groups=Y_GROUPS)  14.9 us
    ppermute x3, waiting for transfers between devices, on_device(): down = lax.ppermute(add(down, own[block])[0], 'tensor', DOWN)  10.8 us
    ppermute x2, starting transfers between devices, on_device(): up = lax.ppermute(add(up, own[block])[0], 'tensor', UP)  5.88 us
    ppermute x1, starting transfers between devices, on_device(): down = lax.ppermute(down, 'tensor', DOWN)  3.62 us
    ppermute x1, waiting for transfers between devices, on_device(): down = lax.ppermute(down, 'tensor', DOWN)  2.04 us
    pallas_call x1, Pallas kernels, on_device(): kernel(end_states, [((len(GROUPS), ROWS, LANES), f32), ((POLES, SUBS, CHA...  1.57 us
    pallas_call x1, Pallas kernels, on_device(): kernel(convolve_project, [(rows, LINK), (rows, LINK), (rows, bf16)], scra...  1.22 us
  transfers between devices with their start and end apart: 7, of which 4 were waited for; matrix products, arithmetic and copies ran while one was open for 0% of the time, Pallas kernels for 1%

profile of v3, /device:TPU:7, one launch (start us, length us, event | category | flops | bytes accessed | tf_op | source)
XLA Modules:
  0.0 59.4 jit_solution(14312430023422916986)
XLA Ops:
  0.0 0.0 copy-start.2
  0.0 1.6 %shard_map.64 = (f32[4,128,128]{2,1,0:T(8,128)S(1)}, f32[16,8,512]{2,1,0:T(8,128)S(1)}, bf16[8,16,512]{2,1,0:T(8,128)(2,1)S(1)}) custom-call(bf16[128,512]{1,0:T(8,128)(2,1)} %gate_hbm.1, bf16[128,512]{1,0:T(8,128)(2,1)} %value_hbm.1, f32[16,512]{1,0:T(8,128)} %rate_ref.3), custom_call_target="tpu_custom_call" | custom-call | flops 8000000000 | bytes 1000000 | tf_op jit(solution)/shard_map/pallas_call | solution.py:150
  1.6 17.6 %all_to_all.10.came_ref = bf16[8,16,512]{2,1,0:T(8,128)(2,1)S(1)} all-to-all(bf16[8,16,512]{2,1,0:T(8,128)(2,1)S(1)} %get-tuple-element.19), channel_id=1, replica_groups={{0,8,16,24,32,40,48,56},{64,72,80,88,96,104,112,120},{128,136,144,152,1..., dimensions={0} | all-to-all | bytes 262144 | tf_op jit(solution)/shard_map/all_to_all | solution.py:162
  19.2 0.0 copy-done.2
  19.2 0.0 copy-start
  19.2 0.0 copy-start.1
  19.2 0.0 copy-start.3
  19.2 0.1 shard_map.65
  19.3 14.9 %all_to_all.11.came_ref = bf16[8,16,512]{2,1,0:T(8,128)(2,1)S(1)} all-to-all(bf16[8,16,512]{2,1,0:T(8,128)(2,1)S(1)} %get-tuple-element.20), channel_id=1, replica_groups={{0,64,128,192,256,320,384,448},{8,72,136,200,264,328,392,456},{16,80,14..., dimensions={0} | all-to-all | bytes 262144 | tf_op jit(solution)/shard_map/all_to_all | solution.py:166
  34.2 0.0 copy-done
  34.2 0.0 copy-done.1
  34.2 0.0 copy-done.3
  34.2 1.2 %shard_map.66 = (bf16[128,512]{1,0:T(8,128)(2,1)S(1)}, bf16[128,512]{1,0:T(8,128)(2,1)S(1)}, bf16[128,512]{1,0:T(8,128)(2,1)S(1)}) custom-call(bf16[8,16,512]{2,1,0:T(8,128)(2,1)S(1)} %all_to_all.11.came_ref, f32[16,512]{1,0:T(8,128)S(1)} %get-tuple-element.21.prior_ref, f32[16,8,512]{2,1,0:T(8,128)S(1)} %get-tuple-element.22.ends_ref, ...), custom_call_target="tpu_custom_call" | custom-call | flops 300000000 | bytes 3000000 | tf_op jit(solution)/shard_map/pallas_call | solution.py:167
  35.4 3.6 %collective-permute-start = (bf16[128,512]{1,0:T(8,128)(2,1)S(1)}, bf16[128,512]{1,0:T(8,128)(2,1)S(1)}, u32[]{:S(2)}, u32[]{:S(2)}) collective-permute-start(bf16[128,512]{1,0:T(8,128)(2,1)S(1)} %get-tuple-element.24), channel_id=1, source_target_pairs={{0,7},{1,0},{2,1},{3,2},{4,3},{5,4},{6,5},{7,6},{8,15},{9,8},{10,9... | collective-permute-start | bytes 393224 | tf_op jit(solution)/shard_map/ppermute | solution.py:173
  39.0 0.1 collective-permute-start.4
  39.2 0.6 shard_map.67
  39.7 2.0 %collective-permute-done.came_ref = bf16[128,512]{1,0:T(8,128)(2,1)S(1)} collective-permute-done((bf16[128,512]{1,0:T(8,128)(2,1)S(1)}, bf16[128,512]{1,0:T(8,128)(2,1)S(1)}, u32[]{:S(2)}, u32[]{:S(2)}) %collective-permute-start) | collective-permute-done | bytes 131104 | tf_op jit(solution)/shard_map/ppermute | solution.py:173
  41.8 0.0 collective-permute-start.1
  41.8 0.0 collective-permute-done.4.came_ref
  41.9 2.9 %collective-permute-start.5 = (bf16[128,512]{1,0:T(8,128)(2,1)S(1)}, bf16[128,512]{1,0:T(8,128)(2,1)S(1)}, u32[]{:S(2)}, u32[]{:S(2)}) collective-permute-start(bf16[128,512]{1,0:T(8,128)(2,1)S(1)} %shard_map.71), channel_id=1, source_target_pairs={{0,1},{1,2},{2,3},{3,4},{4,5},{5,6},{6,7},{7,0},{8,9},{9,10},{10,1... | collective-permute-start | bytes 393224 | tf_op jit(solution)/shard_map/ppermute | solution.py:183
  44.8 2.6 %collective-permute-done.1.came_ref = bf16[128,512]{1,0:T(8,128)(2,1)S(1)} collective-permute-done((bf16[128,512]{1,0:T(8,128)(2,1)S(1)}, bf16[128,512]{1,0:T(8,128)(2,1)S(1)}, u32[]{:S(2)}, u32[]{:S(2)}) %collective-permute-start.1) | collective-permute-done | bytes 131104 | tf_op jit(solution)/shard_map/ppermute | solution.py:181
  47.5 0.0 collective-permute-start.2
  47.5 0.0 collective-permute-done.5.came_ref
  47.5 2.9 %collective-permute-start.6 = (bf16[128,512]{1,0:T(8,128)(2,1)S(1)}, bf16[128,512]{1,0:T(8,128)(2,1)S(1)}, u32[]{:S(2)}, u32[]{:S(2)}) collective-permute-start(bf16[128,512]{1,0:T(8,128)(2,1)S(1)} %shard_map.72), channel_id=1, source_target_pairs={{0,1},{1,2},{2,3},{3,4},{4,5},{5,6},{6,7},{7,0},{8,9},{9,10},{10,1... | collective-permute-start | bytes 393224 | tf_op jit(solution)/shard_map/ppermute | solution.py:183
  50.5 2.6 %collective-permute-done.2.came_ref = bf16[128,512]{1,0:T(8,128)(2,1)S(1)} collective-permute-done((bf16[128,512]{1,0:T(8,128)(2,1)S(1)}, bf16[128,512]{1,0:T(8,128)(2,1)S(1)}, u32[]{:S(2)}, u32[]{:S(2)}) %collective-permute-start.2) | collective-permute-done | bytes 131104 | tf_op jit(solution)/shard_map/ppermute | solution.py:181
  53.1 0.0 collective-permute-start.3
  53.1 0.0 collective-permute-done.6.up_ref
  53.1 5.6 %collective-permute-done.3.down_ref = bf16[128,512]{1,0:T(8,128)(2,1)S(1)} collective-permute-done((bf16[128,512]{1,0:T(8,128)(2,1)S(1)}, bf16[128,512]{1,0:T(8,128)(2,1)S(1)}, u32[]{:S(2)}, u32[]{:S(2)}) %collective-permute-start.3) | collective-permute-done | bytes 131104 | tf_op jit(solution)/shard_map/ppermute | solution.py:181
  58.7 0.7 %shard_map.73 = bf16[128,512]{1,0:T(8,128)(2,1)} custom-call(bf16[128,512]{1,0:T(8,128)(2,1)S(1)} %collective-permute-done.3.down_ref, bf16[128,512]{1,0:T(8,128)(2,1)S(1)} %collective-permute-done.6.up_ref, f32[128,512]{1,0:T(8,128)S(1)} %get-tuple-element.32.own_ref), custom_call_target="tpu_custom_call" | custom-call | flops 200000 | bytes 600000 | tf_op jit(solution)/shard_map/pallas_call | solution.py:184
  (5 shorter events, 0.1 us)
Async XLA Ops:
  0.0 19.2 %copy-start.2 = (f32[16,512]{1,0:T(8,128)S(1)}, f32[16,512]{1,0:T(8,128)}, u32[]{:S(2)}) copy-start(f32[16,512]{1,0:T(8,128)} %rate_ref.3) | copy-start | bytes 98308
  19.2 15.0 %copy-start = (bf16[512,4096]{1,0:T(8,128)(2,1)S(1)}, bf16[512,4096]{1,0:T(8,128)(2,1)}, u32[]{:S(2)}) copy-start(bf16[512,4096]{1,0:T(8,128)(2,1)} %weight_ref.3) | copy-start | bytes 12582916
  19.2 15.0 %copy-start.1 = (bf16[128,512]{1,0:T(8,128)(2,1)S(1)}, bf16[128,512]{1,0:T(8,128)(2,1)}, u32[]{:S(2)}) copy-start(bf16[128,512]{1,0:T(8,128)(2,1)} %query_ref.1) | copy-start | bytes 393220
  19.2 15.0 %copy-start.3 = (f32[16,512]{1,0:T(8,128)S(1)}, f32[16,512]{1,0:T(8,128)}, u32[]{:S(2)}) copy-start(f32[16,512]{1,0:T(8,128)} %residue_ref.1) | copy-start | bytes 98308
  35.4 6.4 %collective-permute-start = (bf16[128,512]{1,0:T(8,128)(2,1)S(1)}, bf16[128,512]{1,0:T(8,128)(2,1)S(1)}, u32[]{:S(2)}, u32[]{:S(2)}) collective-permute-start(bf16[128,512]{1,0:T(8,128)(2,1)S(1)} %get-tuple-element.24), channel_id=1, source_target_pairs={{0,7},{1,0},{2,1},{3,2},{4,3},{5,4},{6,5},{7,6},{8,15},{9,8},{10,9... | collective-permute-start | bytes 393224 | tf_op jit(solution)/shard_map/ppermute | solution.py:173
  39.0 2.8 %collective-permute-start.4 = (bf16[128,512]{1,0:T(8,128)(2,1)S(1)}, bf16[128,512]{1,0:T(8,128)(2,1)S(1)}, u32[]{:S(2)}, u32[]{:S(2)}) collective-permute-start(bf16[128,512]{1,0:T(8,128)(2,1)S(1)} %get-tuple-element.29), channel_id=1, source_target_pairs={{0,1},{1,2},{2,3},{3,4},{4,5},{5,6},{6,7},{7,0},{8,9},{9,10},{10,1... | collective-permute-start | bytes 393224 | tf_op jit(solution)/shard_map/ppermute | solution.py:174
  41.8 5.6 %collective-permute-start.1 = (bf16[128,512]{1,0:T(8,128)(2,1)S(1)}, bf16[128,512]{1,0:T(8,128)(2,1)S(1)}, u32[]{:S(2)}, u32[]{:S(2)}) collective-permute-start(bf16[128,512]{1,0:T(8,128)(2,1)S(1)} %shard_map.68), channel_id=1, source_target_pairs={{0,7},{1,0},{2,1},{3,2},{4,3},{5,4},{6,5},{7,6},{8,15},{9,8},{10,9... | collective-permute-start | bytes 393224 | tf_op jit(solution)/shard_map/ppermute | solution.py:181
  41.9 5.6 %collective-permute-start.5 = (bf16[128,512]{1,0:T(8,128)(2,1)S(1)}, bf16[128,512]{1,0:T(8,128)(2,1)S(1)}, u32[]{:S(2)}, u32[]{:S(2)}) collective-permute-start(bf16[128,512]{1,0:T(8,128)(2,1)S(1)} %shard_map.71), channel_id=1, source_target_pairs={{0,1},{1,2},{2,3},{3,4},{4,5},{5,6},{6,7},{7,0},{8,9},{9,10},{10,1... | collective-permute-start | bytes 393224 | tf_op jit(solution)/shard_map/ppermute | solution.py:183
  47.5 5.6 %collective-permute-start.2 = (bf16[128,512]{1,0:T(8,128)(2,1)S(1)}, bf16[128,512]{1,0:T(8,128)(2,1)S(1)}, u32[]{:S(2)}, u32[]{:S(2)}) collective-permute-start(bf16[128,512]{1,0:T(8,128)(2,1)S(1)} %shard_map.69), channel_id=1, source_target_pairs={{0,7},{1,0},{2,1},{3,2},{4,3},{5,4},{6,5},{7,6},{8,15},{9,8},{10,9... | collective-permute-start | bytes 393224 | tf_op jit(solution)/shard_map/ppermute | solution.py:181
  47.5 5.6 %collective-permute-start.6 = (bf16[128,512]{1,0:T(8,128)(2,1)S(1)}, bf16[128,512]{1,0:T(8,128)(2,1)S(1)}, u32[]{:S(2)}, u32[]{:S(2)}) collective-permute-start(bf16[128,512]{1,0:T(8,128)(2,1)S(1)} %shard_map.72), channel_id=1, source_target_pairs={{0,1},{1,2},{2,3},{3,4},{4,5},{5,6},{6,7},{7,0},{8,9},{9,10},{10,1... | collective-permute-start | bytes 393224 | tf_op jit(solution)/shard_map/ppermute | solution.py:183
  53.1 5.6 %collective-permute-start.3 = (bf16[128,512]{1,0:T(8,128)(2,1)S(1)}, bf16[128,512]{1,0:T(8,128)(2,1)S(1)}, u32[]{:S(2)}, u32[]{:S(2)}) collective-permute-start(bf16[128,512]{1,0:T(8,128)(2,1)S(1)} %shard_map.70), channel_id=1, source_target_pairs={{0,7},{1,0},{2,1},{3,2},{4,3},{5,4},{6,5},{7,6},{8,15},{9,8},{10,9... | collective-permute-start | bytes 393224 | tf_op jit(solution)/shard_map/ppermute | solution.py:181

commit v4 on v2

--- a/solution.py
+++ b/solution.py
@@ -57,34 +57,29 @@
             send_ref[j, :, lanes] = total
 
 
-def chunk_carry(came_ref, rate_ref, prior_ref, send_ref):
-    z = lax.rem(lax.axis_index("context"), RING)
-    shrink = jnp.exp(-rate_ref[...] * (ROWS / SEQ))
+def row_carry(came_ref, rate_ref, send_ref):
+    context = lax.axis_index("context")
+    z, y = lax.rem(context, RING), context // RING
+    shrink = jnp.exp(-rate_ref[...] * (RING * ROWS / SEQ))
     prior = jnp.zeros((POLES, CHANNELS), jnp.float32)
-    total = jnp.zeros((POLES, CHANNELS), jnp.float32)
     for j in range(RING):
-        came = came_ref[j].astype(jnp.float32)
-        prior = jnp.where(j < z, prior * shrink + came, prior)
-        total = total * shrink + came
-    prior_ref[...] = prior
-    sent = total.astype(LINK)
+        prior = jnp.where(j < y, prior * shrink + came_ref[j].astype(jnp.float32), prior)
+    alone = prior.astype(LINK)
+    both = (prior * shrink + came_ref[y].astype(jnp.float32)).astype(LINK)
     for j in range(RING):
-        send_ref[j] = sent
+        send_ref[j] = jnp.where(j > z, both, alone)
 
 
 def convolve_project(
-    came_ref, prior_ref, ends_ref, x_ref, query_ref, residue_ref, rate_ref, weight_ref,
+    came_ref, ends_ref, x_ref, query_ref, residue_ref, rate_ref, weight_ref,
     send_ref, gated_ref, y_ref,
 ):
-    context = lax.axis_index("context")
     core = lax.rem(lax.axis_index("tensor"), 2)
-    z, y = lax.rem(context, RING), context // RING
-    shrink = jnp.exp(-rate_ref[...] * (RING * ROWS / SEQ))
+    z = lax.rem(lax.axis_index("context"), RING)
+    shrink = jnp.exp(-rate_ref[...] * (ROWS / SEQ))
     carry = jnp.zeros((POLES, CHANNELS), jnp.float32)
     for j in range(RING):
-        carry = jnp.where(j < y, carry * shrink + came_ref[j].astype(jnp.float32), carry)
-    behind = (z * ROWS).astype(jnp.float32) / SEQ
-    carry = carry * jnp.exp(-rate_ref[...] * behind) + prior_ref[...]
+        carry = carry * shrink + came_ref[lax.rem(z + j, RING)].astype(jnp.float32)
     for g, lanes in enumerate(GROUPS):
         rate = rate_ref[:, lanes] / SEQ
         steps = over_subs(rate)
@@ -158,18 +153,18 @@
         in_specs=[pl.BlockSpec(memory_space=pltpu.HBM)] * 3,
         flops=8_000_000_000, moved=1_000_000,
     )(*(pltpu.with_memory_space_constraint(a, pltpu.HBM) for a in (key_gate, values, decay_rates)))
+    came = lax.all_to_all(sent, "context", 0, 0, axis_index_groups=Y_GROUPS)
+    (sent,) = kernel(row_carry, [(block, LINK)], flops=8_000_000_000, moved=300_000)(
+        came, decay_rates
+    )
     came = lax.all_to_all(sent, "context", 0, 0, axis_index_groups=Z_GROUPS)
-    prior, sent = kernel(
-        chunk_carry, [(modes, f32), (block, LINK)], flops=8_000_000_000, moved=300_000
-    )(came, decay_rates)
-    came = lax.all_to_all(sent, "context", 0, 0, axis_index_groups=Y_GROUPS)
     halves = (XCHIPS, ROWS, CHANNELS)
     sent, gated = kernel(
         convolve_project,
         [(halves, bf16), (rows, bf16)],
         scratch=[pltpu.VMEM((len(GROUPS), ROWS, LANES), f32)],
         flops=300_000_000, moved=3_000_000,
-    )(came, prior, ends, x, queries, residues, decay_rates, out_weight)
+    )(came, ends, x, queries, residues, decay_rates, out_weight)
     came = lax.ppermute(sent, "tensor", SIBLING)
     (kept,) = kernel(project_own, [(halves, f32)], flops=600_000_000, moved=3_000_000)(
         gated, out_weight

time: 56.9 us -> 56.9 us (level)
  no operation moved by 1% of the time
where the time goes in v4:
time: 56.9 us; the launch traced here: 56.7 us
  blocking collectives  45.8 us (80%)
  starting transfers between devices  5.53 us (10%)
  Pallas kernels  4.25 us (7%)
  waiting for transfers between devices  1.05 us (2%)
    all_to_all x1, blocking collectives, on_device(): came = lax.all_to_all(sent, 'context', 0, 0, axis_index_groups=Z_GROUPS)  18 us
    all_to_all x1, blocking collectives, on_device(): came = lax.all_to_all(sent, 'context', 0, 0, axis_index_groups=Y_GROUPS)  15.4 us
    all_to_all x1, blocking collectives, on_device(): came = lax.all_to_all(pair, 'tensor', 0, 0, axis_index_groups=X_GROUPS)  12.4 us
    ppermute x1, starting transfers between devices, on_device(): came = lax.ppermute(sent, 'tensor', SIBLING)  5.53 us
    pallas_call x1, Pallas kernels, on_device(): kernel(end_states, [((len(GROUPS), ROWS, LANES), f32), ((POLES, SUBS, CHA...  1.57 us
    pallas_call x1, Pallas kernels, on_device(): kernel(convolve_project, [(halves, bf16), (rows, bf16)], scratch=[pltpu.V...  1.34 us
  transfers between devices with their start and end apart: 1, of which 1 were waited for; matrix products, arithmetic and copies ran while one was open for 0% of the time, Pallas kernels for 1%

profile of v4, /device:TPU:1, one launch (start us, length us, event | category | flops | bytes accessed | tf_op | source)
XLA Modules:
  0.0 56.7 jit_solution(11033250492449929722)
XLA Ops:
  0.0 0.0 copy-start.2
  0.0 1.6 %shard_map.64 = (f32[4,128,128]{2,1,0:T(8,128)S(1)}, f32[16,8,512]{2,1,0:T(8,128)S(1)}, bf16[8,16,512]{2,1,0:T(8,128)(2,1)S(1)}) custom-call(bf16[128,512]{1,0:T(8,128)(2,1)} %gate_hbm.1, bf16[128,512]{1,0:T(8,128)(2,1)} %value_hbm.1, f32[16,512]{1,0:T(8,128)} %rate_ref.3), custom_call_target="tpu_custom_call" | custom-call | flops 8000000000 | bytes 1000000 | tf_op jit(solution)/shard_map/pallas_call | solution.py:144
  1.6 15.4 %all_to_all.15.came_ref = bf16[8,16,512]{2,1,0:T(8,128)(2,1)S(1)} all-to-all(bf16[8,16,512]{2,1,0:T(8,128)(2,1)S(1)} %get-tuple-element.10), channel_id=1, replica_groups={{0,64,128,192,256,320,384,448},{8,72,136,200,264,328,392,456},{16,80,14..., dimensions={0} | all-to-all | bytes 262144 | tf_op jit(solution)/shard_map/all_to_all | solution.py:156
  17.0 0.0 copy-done.2
  17.0 0.0 copy-start
  17.0 0.0 copy-start.1
  17.0 0.0 copy-start.3
  17.0 0.1 shard_map.65
  17.0 18.0 %all_to_all.16.came_ref = bf16[8,16,512]{2,1,0:T(8,128)(2,1)S(1)} all-to-all(bf16[8,16,512]{2,1,0:T(8,128)(2,1)S(1)} %shard_map.65), channel_id=1, replica_groups={{0,8,16,24,32,40,48,56},{64,72,80,88,96,104,112,120},{128,136,144,152,1..., dimensions={0} | all-to-all | bytes 262144 | tf_op jit(solution)/shard_map/all_to_all | solution.py:160
  35.0 0.0 copy-done
  35.0 0.0 copy-done.1
  35.0 0.0 copy-done.3
  35.0 1.3 %shard_map.66 = (bf16[4,128,512]{2,1,0:T(8,128)(2,1)S(1)}, bf16[128,512]{1,0:T(8,128)(2,1)S(1)}) custom-call(bf16[8,16,512]{2,1,0:T(8,128)(2,1)S(1)} %all_to_all.16.came_ref, f32[16,8,512]{2,1,0:T(8,128)S(1)} %get-tuple-element.11.ends_ref, f32[4,128,128]{2,1,0:T(8,128)S(1)} %get-tuple-element.12.x_ref, bf16[128,512]{1,0:T(8,128)(2,1)S(1)} %copy-done.1, ...), custom_call_target="tpu_custom_call" | custom-call | flops 300000000 | bytes 3000000 | tf_op jit(solution)/shard_map/pallas_call | solution.py:162
  36.4 5.5 %collective-permute-start = (bf16[4,128,512]{2,1,0:T(8,128)(2,1)S(1)}, bf16[4,128,512]{2,1,0:T(8,128)(2,1)S(1)}, u32[]{:S(2)}, u32[]{:S(2)}) collective-permute-start(bf16[4,128,512]{2,1,0:T(8,128)(2,1)S(1)} %get-tuple-element.14), channel_id=1, source_target_pairs={{0,1},{1,0},{2,3},{3,2},{4,5},{5,4},{6,7},{7,6},{8,9},{9,8},{10,11... | collective-permute-start | bytes 1572872 | tf_op jit(solution)/shard_map/ppermute | solution.py:168
  41.9 0.5 shard_map.67.kept_ref
  42.4 1.1 %collective-permute-done.came_ref = bf16[4,128,512]{2,1,0:T(8,128)(2,1)S(1)} collective-permute-done((bf16[4,128,512]{2,1,0:T(8,128)(2,1)S(1)}, bf16[4,128,512]{2,1,0:T(8,128)(2,1)S(1)}, u32[]{:S(2)}, u32[]{:S(2)}) %collective-permute-start) | collective-permute-done | bytes 524320 | tf_op jit(solution)/shard_map/ppermute | solution.py:168
  43.4 0.1 shard_map.68
  43.5 12.4 %all_to_all.17.came_ref = bf16[4,128,512]{2,1,0:T(8,128)(2,1)S(1)} all-to-all(bf16[4,128,512]{2,1,0:T(8,128)(2,1)S(1)} %shard_map.68), channel_id=1, replica_groups={{0,2,4,6},{1,3,5,7},{8,10,12,14},{9,11,13,15},{16,18,20,22},{17,19,21,2..., dimensions={0} | all-to-all | bytes 1048576 | tf_op jit(solution)/shard_map/all_to_all | solution.py:173
  56.0 0.7 %shard_map.69 = bf16[128,512]{1,0:T(8,128)(2,1)} custom-call(bf16[4,128,512]{2,1,0:T(8,128)(2,1)S(1)} %all_to_all.17.came_ref), custom_call_target="tpu_custom_call" | custom-call | flops 300000 | bytes 700000 | tf_op jit(solution)/shard_map/pallas_call | solution.py:174
Async XLA Ops:
  0.0 17.0 %copy-start.2 = (f32[16,512]{1,0:T(8,128)S(1)}, f32[16,512]{1,0:T(8,128)}, u32[]{:S(2)}) copy-start(f32[16,512]{1,0:T(8,128)} %rate_ref.3) | copy-start | bytes 98308
  17.0 18.1 %copy-start = (bf16[512,4096]{1,0:T(8,128)(2,1)S(1)}, bf16[512,4096]{1,0:T(8,128)(2,1)}, u32[]{:S(2)}) copy-start(bf16[512,4096]{1,0:T(8,128)(2,1)} %weight_ref.3) | copy-start | bytes 12582916
  17.0 18.1 %copy-start.1 = (bf16[128,512]{1,0:T(8,128)(2,1)S(1)}, bf16[128,512]{1,0:T(8,128)(2,1)}, u32[]{:S(2)}) copy-start(bf16[128,512]{1,0:T(8,128)(2,1)} %query_ref.1) | copy-start | bytes 393220
  17.0 18.1 %copy-start.3 = (f32[16,512]{1,0:T(8,128)S(1)}, f32[16,512]{1,0:T(8,128)}, u32[]{:S(2)}) copy-start(f32[16,512]{1,0:T(8,128)} %residue_ref.1) | copy-start | bytes 98308
  36.4 7.1 %collective-permute-start = (bf16[4,128,512]{2,1,0:T(8,128)(2,1)S(1)}, bf16[4,128,512]{2,1,0:T(8,128)(2,1)S(1)}, u32[]{:S(2)}, u32[]{:S(2)}) collective-permute-start(bf16[4,128,512]{2,1,0:T(8,128)(2,1)S(1)} %get-tuple-element.14), channel_id=1, source_target_pairs={{0,1},{1,0},{2,3},{3,2},{4,5},{5,4},{6,7},{7,6},{8,9},{9,8},{10,11... | collective-permute-start | bytes 1572872 | tf_op jit(solution)/shard_map/ppermute | solution.py:168

commit v5 on v4

--- a/solution.py
+++ b/solution.py
@@ -20,7 +20,7 @@
 Z_GROUPS = [[y * RING + z for z in range(RING)] for y in range(RING)]
 Y_GROUPS = [[y * RING + z for y in range(RING)] for z in range(RING)]
 X_GROUPS = [[x * 2 + core for x in range(XCHIPS)] for core in range(2)]
-SIBLING = [(t, t ^ 1) for t in range(2 * XCHIPS)]
+CORE_GROUPS = [[2 * x, 2 * x + 1] for x in range(XCHIPS)]
 
 
 def over_subs(rows):
@@ -31,12 +31,25 @@
     return lax.broadcasted_iota(jnp.int32, (POLES, SUBS, LANES), 1).astype(jnp.float32)
 
 
+def weight_copies(weight_hbm, weight_ref, sems):
+    core = lax.rem(lax.axis_index("tensor"), 2)
+    copies = []
+    for chip in range(XCHIPS):
+        columns = pl.ds(pl.multiple_of((2 * chip + core) * CHANNELS, CHANNELS), CHANNELS)
+        copies.append(
+            pltpu.make_async_copy(weight_hbm.at[:, columns], weight_ref.at[chip], sems.at[chip])
+        )
+    return copies
+
+
 def end_states(
-    gate_hbm, value_hbm, rate_hbm, x_ref, ends_ref, send_ref, gate_ref, value_ref, rate_ref, sems
+    gate_hbm, value_hbm, rate_hbm, weight_hbm, x_ref, ends_ref, send_ref, weight_ref,
+    gate_ref, value_ref, rate_ref, sems, weight_sems,
 ):
     pairs = ((gate_hbm, gate_ref), (value_hbm, value_ref), (rate_hbm, rate_ref))
     copies = [pltpu.make_async_copy(a, b, sems.at[i]) for i, (a, b) in enumerate(pairs)]
-    for copy in copies:
+    later = weight_copies(weight_hbm, weight_ref, weight_sems)
+    for copy in copies + later:
         copy.start()
     for copy in copies:
         copy.wait()
@@ -55,6 +68,8 @@
         total = jnp.sum(state * jnp.exp(-over_subs(rate) * left), axis=1).astype(LINK)
         for j in range(RING):
             send_ref[j, :, lanes] = total
+    for copy in later:
+        copy.wait()
 
 
 def row_carry(came_ref, rate_ref, send_ref):
@@ -70,11 +85,14 @@
         send_ref[j] = jnp.where(j > z, both, alone)
 
 
-def convolve_project(
-    came_ref, ends_ref, x_ref, query_ref, residue_ref, rate_ref, weight_ref,
-    send_ref, gated_ref, y_ref,
+def convolve_gate(
+    came_ref, ends_ref, x_ref, query_ref, residue_ref, rate_ref, weights_hbm,
+    gated_ref, weight_ref, y_ref, sems,
 ):
     core = lax.rem(lax.axis_index("tensor"), 2)
+    copies = weight_copies(weights_hbm.at[1 - core], weight_ref, sems)
+    for copy in copies:
+        copy.start()
     z = lax.rem(lax.axis_index("context"), RING)
     shrink = jnp.exp(-rate_ref[...] * (ROWS / SEQ))
     carry = jnp.zeros((POLES, CHANNELS), jnp.float32)
@@ -96,27 +114,20 @@
             state = shrink_one * state + row[None]
             y_ref[g, pl.ds(t, SUBS, stride=STEPS), :] = jnp.sum(residue * state, axis=0)
     convolved = jnp.concatenate([y_ref[g] for g in range(len(GROUPS))], axis=1)
-    gated = (query_ref[...].astype(jnp.float32) * convolved).astype(jnp.bfloat16)
-    gated_ref[...] = gated
-    project(gated, weight_ref, 1 - core, send_ref)
-
-
-def project(gated, weight_ref, core, out_ref):
+    gated = query_ref[...].astype(jnp.float32) * convolved
+    gated_ref[...] = gated.astype(jnp.bfloat16)
+    for copy in copies:
+        copy.wait()
+
+
+def project(gated_ref, weight_ref, sibling_ref, out_ref):
+    core = lax.rem(lax.axis_index("tensor"), 2)
+    mine, other = gated_ref[core], gated_ref[1 - core]
     for chip in range(XCHIPS):
-        column = pl.multiple_of((2 * chip + core) * CHANNELS, CHANNELS)
         partial = jnp.dot(
-            gated, weight_ref[:, pl.ds(column, CHANNELS)], preferred_element_type=jnp.float32
-        )
+            mine, weight_ref[chip], preferred_element_type=jnp.float32
+        ) + jnp.dot(other, sibling_ref[chip], preferred_element_type=jnp.float32)
         out_ref[chip] = partial.astype(out_ref.dtype)
-
-
-def project_own(gated_ref, weight_ref, keep_ref):
-    project(gated_ref[...], weight_ref, lax.rem(lax.axis_index("tensor"), 2), keep_ref)
-
-
-def add_pair(kept_ref, came_ref, out_ref):
-    total = kept_ref[...].astype(jnp.float32) + came_ref[...].astype(jnp.float32)
-    out_ref[...] = total.astype(out_ref.dtype)
 
 
 def add_chips(came_ref, out_ref):
@@ -137,39 +148,58 @@
     )
 
 
+def in_hbm(array):
+    return pltpu.with_memory_space_constraint(array, pltpu.HBM)
+
+
 def on_device(queries, key_gate, values, residues, decay_rates, out_weight):
     f32, bf16 = jnp.float32, jnp.bfloat16
     block = (RING, POLES, CHANNELS)
     rows, modes = (ROWS, CHANNELS), (POLES, CHANNELS)
-    x, ends, sent = kernel(
+    columns = (XCHIPS, CHANNELS, CHANNELS)
+    weights = lax.all_gather(out_weight, "tensor", axis_index_groups=CORE_GROUPS)
+    x, ends, sent, own = kernel(
         end_states,
-        [((len(GROUPS), ROWS, LANES), f32), ((POLES, SUBS, CHANNELS), f32), (block, LINK)],
+        [
+            ((len(GROUPS), ROWS, LANES), f32),
+            ((POLES, SUBS, CHANNELS), f32),
+            (block, LINK),
+            (columns, bf16),
+        ],
         scratch=[
             pltpu.VMEM(rows, bf16),
             pltpu.VMEM(rows, bf16),
             pltpu.VMEM(modes, f32),
             pltpu.SemaphoreType.DMA((3,)),
+            pltpu.SemaphoreType.DMA((XCHIPS,)),
         ],
-        in_specs=[pl.BlockSpec(memory_space=pltpu.HBM)] * 3,
+        in_specs=[pl.BlockSpec(memory_space=pltpu.HBM)] * 4,
         flops=8_000_000_000, moved=1_000_000,
-    )(*(pltpu.with_memory_space_constraint(a, pltpu.HBM) for a in (key_gate, values, decay_rates)))
+    )(*map(in_hbm, (key_gate, values, decay_rates, out_weight)))
     came = lax.all_to_all(sent, "context", 0, 0, axis_index_groups=Y_GROUPS)
     (sent,) = kernel(row_carry, [(block, LINK)], flops=8_000_000_000, moved=300_000)(
         came, decay_rates
     )
     came = lax.all_to_all(sent, "context", 0, 0, axis_index_groups=Z_GROUPS)
     halves = (XCHIPS, ROWS, CHANNELS)
-    sent, gated = kernel(
-        convolve_project,
-        [(halves, bf16), (rows, bf16)],
-        scratch=[pltpu.VMEM((len(GROUPS), ROWS, LANES), f32)],
-        flops=300_000_000, moved=3_000_000,
-    )(came, ends, x, queries, residues, decay_rates, out_weight)
-    came = lax.ppermute(sent, "tensor", SIBLING)
-    (kept,) = kernel(project_own, [(halves, f32)], flops=600_000_000, moved=3_000_000)(
-        gated, out_weight
-    )
-    (pair,) = kernel(add_pair, [(halves, bf16)], flops=300_000, moved=1_500_000)(kept, came)
+    gated, sibling = kernel(
+        convolve_gate,
+        [(rows, bf16), (columns, bf16)],
+        scratch=[
+            pltpu.VMEM((len(GROUPS), ROWS, LANES), f32),
+            pltpu.SemaphoreType.DMA((XCHIPS,)),
+        ],
+        in_specs=[pl.BlockSpec(memory_space=pltpu.VMEM)] * 6
+        + [pl.BlockSpec(memory_space=pltpu.HBM)],
+        flops=100_000, moved=10_000,
+    )(
+        came, ends, x, queries, residues, decay_rates,
+        in_hbm(weights),
+    )
+    both = lax.all_gather(gated, "tensor", axis_index_groups=CORE_GROUPS)
+    (pair,) = kernel(project, [(halves, bf16)], flops=600_000_000, moved=5_000_000)(
+        both, own, sibling
+    )
     came = lax.all_to_all(pair, "tensor", 0, 0, axis_index_groups=X_GROUPS)
     (mixed,) = kernel(add_chips, [(rows, bf16)], flops=300_000, moved=700_000)(came)
     return mixed

time: 56.9 us -> 70.5 us (1.24)
  between operations: 0.06 us -> 13.4 us
  starting transfers between devices: 5.53 us -> 0.01 us
  blocking collectives: 45.8 us -> 49.1 us
  waiting for transfers between devices: 1.05 us -> 2.55 us
  Pallas kernels: 4.25 us -> 5.16 us
    ppermute x1 -> x0, starting transfers between devices: 5.53 us -> none  [on_device(): came = lax.ppermute(sent, 'tensor', SIBLING)]
    all_gather x0 -> x1, blocking collectives: none -> 3.52 us  [on_device(): both = lax.all_gather(gated, 'tensor', axis_index_groups=CORE_GROUPS)]
    all_gather x0 -> x1, waiting for transfers between devices: none -> 1.84 us  [on_device(): lax.all_gather(out_weight, 'tensor', axis_index_groups=CORE_GROUPS)]
    ppermute x1 -> x0, waiting for transfers between devices: 1.05 us -> none  [on_device(): came = lax.ppermute(sent, 'tensor', SIBLING)]
    unnamed x0 -> x1, waiting for transfers between devices: none -> 0.71 us
    pallas_call x3 -> x2, Pallas kernels: 1.89 us -> 2.28 us  [the longest x1 1.57 us: on_device(): kernel(convolve_gate, [(rows, bf16), (columns, bf16)], scratch=[pltpu.VME...]
  transfers between devices with their start and end apart: 1 -> 1, of which waited for: 1 -> 1; matrix products, arithmetic and copies ran while one was open for 0% -> 0% of each run, Pallas kernels for 1% -> 3%
where the time goes in v5:
time: 70.5 us; the launch traced here: 70.3 us
  blocking collectives  49.1 us (70%)
  between operations  13.4 us (19%)
  Pallas kernels  5.16 us (7%)
  waiting for transfers between devices  2.55 us (4%)
    all_to_all x1, blocking collectives, on_device(): came = lax.all_to_all(sent, 'context', 0, 0, axis_index_groups=Z_GROUPS)  17.7 us
    all_to_all x1, blocking collectives, on_device(): came = lax.all_to_all(sent, 'context', 0, 0, axis_index_groups=Y_GROUPS)  15.4 us
    all_to_all x1, blocking collectives, on_device(): came = lax.all_to_all(pair, 'tensor', 0, 0, axis_index_groups=X_GROUPS)  12.4 us
    all_gather x1, blocking collectives, on_device(): both = lax.all_gather(gated, 'tensor', axis_index_groups=CORE_GROUPS)  3.52 us
    pallas_call x1, Pallas kernels, on_device(): kernel(end_states, [((len(GROUPS), ROWS, LANES), f32), ((POLES, SUBS, CHA...  2.09 us
    all_gather x1, waiting for transfers between devices, on_device(): lax.all_gather(out_weight, 'tensor', axis_index_groups=CORE_GROUPS)  1.84 us
    pallas_call x1, Pallas kernels, on_device(): kernel(convolve_gate, [(rows, bf16), (columns, bf16)], scratch=[pltpu.VME...  1.57 us
  transfers between devices with their start and end apart: 1, of which 1 were waited for; matrix products, arithmetic and copies ran while one was open for 0% of the time, Pallas kernels for 3%

profile of v5, /device:TPU:1, one launch (start us, length us, event | category | flops | bytes accessed | tf_op | source)
XLA Modules:
  0.0 70.3 jit_solution(7018208695825560780)
XLA Ops:
  6.5 0.0 all-gather.4.cloned.1.call-start
  6.5 0.7 %all-gather.4.cloned.1.call-update = ((bf16[512,4096]{1,0:T(8,128)(2,1)}), bf16[1024,4096]{1,0:T(8,128)(2,1)}) async-update(((), (), s32[]{:S(2)}) %all-gather.4.cloned.1.call-start, bf16[512,4096]{1,0:T(8,128)(2,1)} %weight_hbm.1) | async-update | bytes 16777240
  7.3 0.0 copy-start.1
  7.3 2.1 %shard_map.64 = (f32[4,128,128]{2,1,0:T(8,128)S(1)}, f32[16,8,512]{2,1,0:T(8,128)S(1)}, bf16[8,16,512]{2,1,0:T(8,128)(2,1)S(1)}, bf16[4,512,512]{2,1,0:T(8,128)(2,1)S(1)}) custom-call(bf16[128,512]{1,0:T(8,128)(2,1)} %gate_hbm.1, bf16[128,512]{1,0:T(8,128)(2,1)} %value_hbm.1, f32[16,512]{1,0:T(8,128)} %rate_ref.3, bf16[512,4096]{1,0:T(8,128)(2,1)} %weight_hbm.1), custom_call_target="tpu_custom_call" | custom-call | flops 8000000000 | bytes 1000000 | tf_op jit(solution)/shard_map/pallas_call | solution.py:161
  9.4 15.4 %all_to_all.15.came_ref = bf16[8,16,512]{2,1,0:T(8,128)(2,1)S(1)} all-to-all(bf16[8,16,512]{2,1,0:T(8,128)(2,1)S(1)} %get-tuple-element.11), channel_id=1, replica_groups={{0,64,128,192,256,320,384,448},{8,72,136,200,264,328,392,456},{16,80,14..., dimensions={0} | all-to-all | bytes 262144 | tf_op jit(solution)/shard_map/all_to_all | solution.py:179
  24.7 0.0 copy-done.1
  24.7 0.0 copy-start
  24.7 0.0 copy-start.2
  24.7 0.1 shard_map.65
  24.8 17.7 %all_to_all.16.came_ref = bf16[8,16,512]{2,1,0:T(8,128)(2,1)S(1)} all-to-all(bf16[8,16,512]{2,1,0:T(8,128)(2,1)S(1)} %shard_map.65), channel_id=1, replica_groups={{0,8,16,24,32,40,48,56},{64,72,80,88,96,104,112,120},{128,136,144,152,1..., dimensions={0} | all-to-all | bytes 262144 | tf_op jit(solution)/shard_map/all_to_all | solution.py:183
  42.6 1.8 %all-gather.4.cloned.1.call-done = bf16[1024,4096]{1,0:T(8,128)(2,1)} async-done(((bf16[512,4096]{1,0:T(8,128)(2,1)}), bf16[1024,4096]{1,0:T(8,128)(2,1)}) %all-gather.4.cloned.1.call-update) | async-done | bytes 8388624 | tf_op jit(solution)/shard_map/all_gather | solution.py:160
  44.4 0.0 copy-done
  44.4 0.0 copy-done.2
  44.4 1.6 %shard_map.66 = (bf16[128,512]{1,0:T(8,128)(2,1)S(1)}, bf16[4,512,512]{2,1,0:T(8,128)(2,1)S(1)}) custom-call(bf16[8,16,512]{2,1,0:T(8,128)(2,1)S(1)} %all_to_all.16.came_ref, f32[16,8,512]{2,1,0:T(8,128)S(1)} %get-tuple-element.12.ends_ref, f32[4,128,128]{2,1,0:T(8,128)S(1)} %get-tuple-element.13.x_ref, bf16[128,512]{1,0:T(8,128)(2,1)S(1)} %copy-done, ...), custom_call_target="tpu_custom_call" | custom-call | flops 100000 | bytes 10000 | tf_op jit(solution)/shard_map/pallas_call | solution.py:185
  46.0 3.5 %all-gather.1 = bf16[256,512]{1,0:T(8,128)(2,1)S(1)} all-gather(bf16[128,512]{1,0:T(8,128)(2,1)S(1)} %get-tuple-element.14), channel_id=3, replica_groups={{0,1},{2,3},{4,5},{6,7},{8,9},{10,11},{12,13},{14,15},{16,17},{18,19},{..., dimensions={0}, use_global_device_ids=true | all-gather | bytes 393216 | tf_op jit(solution)/shard_map/all_gather | solution.py:199
  49.5 0.7 %shard_map.67 = bf16[4,128,512]{2,1,0:T(8,128)(2,1)S(1)} custom-call(bf16[2,128,512]{2,1,0:T(8,128)(2,1)S(1)} %bitcast.2, bf16[4,512,512]{2,1,0:T(8,128)(2,1)S(1)} %get-tuple-element.15.weight_ref, bf16[4,512,512]{2,1,0:T(8,128)(2,1)S(1)} %get-tuple-element.16.sibling_ref), custom_call_target="tpu_custom_call" | custom-call | flops 600000000 | bytes 5000000 | tf_op jit(solution)/shard_map/pallas_call | solution.py:200
  50.2 12.4 %all_to_all.17.came_ref = bf16[4,128,512]{2,1,0:T(8,128)(2,1)S(1)} all-to-all(bf16[4,128,512]{2,1,0:T(8,128)(2,1)S(1)} %shard_map.67), channel_id=1, replica_groups={{0,2,4,6},{1,3,5,7},{8,10,12,14},{9,11,13,15},{16,18,20,22},{17,19,21,2..., dimensions={0} | all-to-all | bytes 1048576 | tf_op jit(solution)/shard_map/all_to_all | solution.py:203
  62.7 0.7 %shard_map.68 = bf16[128,512]{1,0:T(8,128)(2,1)} custom-call(bf16[4,128,512]{2,1,0:T(8,128)(2,1)S(1)} %all_to_all.17.came_ref), custom_call_target="tpu_custom_call" | custom-call | flops 300000 | bytes 700000 | tf_op jit(solution)/shard_map/pallas_call | solution.py:204
Async XLA Ops:
  6.5 37.9 %all-gather.4.cloned.1.call-start = ((), (), s32[]{:S(2)}) async-start(), calls=%async_computation.3 | async-start | bytes 12582912 | tf_op jit(solution)/shard_map/all_gather | solution.py:160
  7.3 17.5 %copy-start.1 = (f32[16,512]{1,0:T(8,128)S(1)}, f32[16,512]{1,0:T(8,128)}, u32[]{:S(2)}) copy-start(f32[16,512]{1,0:T(8,128)} %rate_ref.3) | copy-start | bytes 98308
  24.7 19.7 %copy-start = (bf16[128,512]{1,0:T(8,128)(2,1)S(1)}, bf16[128,512]{1,0:T(8,128)(2,1)}, u32[]{:S(2)}) copy-start(bf16[128,512]{1,0:T(8,128)(2,1)} %query_ref.1) | copy-start | bytes 393220
  24.7 19.7 %copy-start.2 = (f32[16,512]{1,0:T(8,128)S(1)}, f32[16,512]{1,0:T(8,128)}, u32[]{:S(2)}) copy-start(f32[16,512]{1,0:T(8,128)} %residue_ref.1) | copy-start | bytes 98308
Sparse Core Ops, SparseCore 0:
  9.4 34.9 all-gather.3

commit v6 on v4

--- a/solution.py
+++ b/solution.py
@@ -20,7 +20,10 @@
 Z_GROUPS = [[y * RING + z for z in range(RING)] for y in range(RING)]
 Y_GROUPS = [[y * RING + z for y in range(RING)] for z in range(RING)]
 X_GROUPS = [[x * 2 + core for x in range(XCHIPS)] for core in range(2)]
-SIBLING = [(t, t ^ 1) for t in range(2 * XCHIPS)]
+CORE_GROUPS = [[2 * x, 2 * x + 1] for x in range(XCHIPS)]
+TENSOR = 2 * XCHIPS
+UP = [(t, (t + 1) % TENSOR) for t in range(TENSOR)]
+DOWN = [(t, (t - 1) % TENSOR) for t in range(TENSOR)]
 
 
 def over_subs(rows):
@@ -70,11 +73,9 @@
         send_ref[j] = jnp.where(j > z, both, alone)
 
 
-def convolve_project(
-    came_ref, ends_ref, x_ref, query_ref, residue_ref, rate_ref, weight_ref,
-    send_ref, gated_ref, y_ref,
+def convolve_gate(
+    came_ref, ends_ref, x_ref, query_ref, residue_ref, rate_ref, gated_ref, y_ref,
 ):
-    core = lax.rem(lax.axis_index("tensor"), 2)
     z = lax.rem(lax.axis_index("context"), RING)
     shrink = jnp.exp(-rate_ref[...] * (ROWS / SEQ))
     carry = jnp.zeros((POLES, CHANNELS), jnp.float32)
@@ -96,27 +97,23 @@
             state = shrink_one * state + row[None]
             y_ref[g, pl.ds(t, SUBS, stride=STEPS), :] = jnp.sum(residue * state, axis=0)
     convolved = jnp.concatenate([y_ref[g] for g in range(len(GROUPS))], axis=1)
-    gated = (query_ref[...].astype(jnp.float32) * convolved).astype(jnp.bfloat16)
-    gated_ref[...] = gated
-    project(gated, weight_ref, 1 - core, send_ref)
+    gated = query_ref[...].astype(jnp.float32) * convolved
+    gated_ref[...] = gated.astype(jnp.bfloat16)
 
 
-def project(gated, weight_ref, core, out_ref):
-    for chip in range(XCHIPS):
-        column = pl.multiple_of((2 * chip + core) * CHANNELS, CHANNELS)
-        partial = jnp.dot(
-            gated, weight_ref[:, pl.ds(column, CHANNELS)], preferred_element_type=jnp.float32
-        )
-        out_ref[chip] = partial.astype(out_ref.dtype)
+def project(gated_ref, weight_ref, up_ref, down_ref, out_ref):
+    for core, sibling_ref in ((0, down_ref), (1, up_ref)):
 
-
-def project_own(gated_ref, weight_ref, keep_ref):
-    project(gated_ref[...], weight_ref, lax.rem(lax.axis_index("tensor"), 2), keep_ref)
-
-
-def add_pair(kept_ref, came_ref, out_ref):
-    total = kept_ref[...].astype(jnp.float32) + came_ref[...].astype(jnp.float32)
-    out_ref[...] = total.astype(out_ref.dtype)
+        @pl.when(lax.rem(lax.axis_index("tensor"), 2) == core)
+        def _():
+            for chip in range(XCHIPS):
+                columns = pl.ds((2 * chip + core) * CHANNELS, CHANNELS)
+                partial = jnp.dot(
+                    gated_ref[core], weight_ref[:, columns], preferred_element_type=jnp.float32
+                ) + jnp.dot(
+                    gated_ref[1 - core], sibling_ref[:, columns], preferred_element_type=jnp.float32
+                )
+                out_ref[chip] = partial.astype(out_ref.dtype)
 
 
 def add_chips(came_ref, out_ref):
@@ -140,6 +137,8 @@
 def on_device(queries, key_gate, values, residues, decay_rates, out_weight):
     f32, bf16 = jnp.float32, jnp.bfloat16
     block = (RING, POLES, CHANNELS)
+    up = lax.ppermute(out_weight, "tensor", UP)
+    down = lax.ppermute(out_weight, "tensor", DOWN)
     rows, modes = (ROWS, CHANNELS), (POLES, CHANNELS)
     x, ends, sent = kernel(
         end_states,
@@ -159,17 +158,16 @@
     )
     came = lax.all_to_all(sent, "context", 0, 0, axis_index_groups=Z_GROUPS)
     halves = (XCHIPS, ROWS, CHANNELS)
-    sent, gated = kernel(
-        convolve_project,
-        [(halves, bf16), (rows, bf16)],
+    (gated,) = kernel(
+        convolve_gate,
+        [(rows, bf16)],
         scratch=[pltpu.VMEM((len(GROUPS), ROWS, LANES), f32)],
-        flops=300_000_000, moved=3_000_000,
-    )(came, ends, x, queries, residues, decay_rates, out_weight)
-    came = lax.ppermute(sent, "tensor", SIBLING)
-    (kept,) = kernel(project_own, [(halves, f32)], flops=600_000_000, moved=3_000_000)(
-        gated, out_weight
+        flops=100_000, moved=10_000,
+    )(came, ends, x, queries, residues, decay_rates)
+    both = lax.all_gather(gated, "tensor", axis_index_groups=CORE_GROUPS)
+    (pair,) = kernel(project, [(halves, bf16)], flops=600_000_000, moved=5_000_000)(
+        both, out_weight, up, down
     )
-    (pair,) = kernel(add_pair, [(halves, bf16)], flops=300_000, moved=1_500_000)(kept, came)
     came = lax.all_to_all(pair, "tensor", 0, 0, axis_index_groups=X_GROUPS)
     (mixed,) = kernel(add_chips, [(rows, bf16)], flops=300_000, moved=700_000)(came)
     return mixed

time: 56.9 us -> 70.5 us (1.24)
  blocking collectives: 45.8 us -> 52.5 us
  waiting for transfers between devices: 1.05 us -> 6.88 us
  starting transfers between devices: 5.53 us -> 6.88 us
    all_gather x0 -> x1, blocking collectives: none -> 6.15 us  [on_device(): both = lax.all_gather(gated, 'tensor', axis_index_groups=CORE_GROUPS)]
    ppermute x1 -> x2, waiting for transfers between devices: 1.05 us -> 6.88 us  [the longest x1 4.21 us: on_device(): up = lax.ppermute(out_weight, 'tensor', UP)]
    all_to_all x1, blocking collectives: 12.4 us -> 17.8 us  [on_device(): came = lax.all_to_all(pair, 'tensor', 0, 0, axis_index_groups=X_GROUPS)]
    all_to_all x1, blocking collectives: 15.4 us -> 10.3 us  [on_device(): came = lax.all_to_all(sent, 'context', 0, 0, axis_index_groups=Y_GROUPS)]
    ppermute x1 -> x2, starting transfers between devices: 5.53 us -> 6.88 us  [the longest x1 4.28 us: on_device(): down = lax.ppermute(out_weight, 'tensor', DOWN)]
    pallas_call x3 -> x2, Pallas kernels: 1.89 us -> 1.68 us  [the longest x1 0.96 us: on_device(): kernel(convolve_gate, [(rows, bf16)], scratch=[pltpu.VMEM((len(GROUPS), R...]
  transfers between devices with their start and end apart: 1 -> 2, of which waited for: 1 -> 2; matrix products, arithmetic and copies ran while one was open for 0% -> 0% of each run, Pallas kernels for 1% -> 4%
where the time goes in v6:
time: 70.5 us; the launch traced here: 70.3 us
  blocking collectives  52.5 us (74%)
  starting transfers between devices  6.88 us (10%)
  waiting for transfers between devices  6.88 us (10%)
  Pallas kernels  4.03 us (6%)
    all_to_all x1, blocking collectives, on_device(): came = lax.all_to_all(sent, 'context', 0, 0, axis_index_groups=Z_GROUPS)  18.2 us
    all_to_all x1, blocking collectives, on_device(): came = lax.all_to_all(pair, 'tensor', 0, 0, axis_index_groups=X_GROUPS)  17.8 us
    all_to_all x1, blocking collectives, on_device(): came = lax.all_to_all(sent, 'context', 0, 0, axis_index_groups=Y_GROUPS)  10.3 us
    all_gather x1, blocking collectives, on_device(): both = lax.all_gather(gated, 'tensor', axis_index_groups=CORE_GROUPS)  6.15 us
    ppermute x1, starting transfers between devices, on_device(): down = lax.ppermute(out_weight, 'tensor', DOWN)  4.28 us
    ppermute x1, waiting for transfers between devices, on_device(): up = lax.ppermute(out_weight, 'tensor', UP)  4.21 us
    ppermute x1, waiting for transfers between devices, on_device(): down = lax.ppermute(out_weight, 'tensor', DOWN)  2.67 us
    ppermute x1, starting transfers between devices, on_device(): up = lax.ppermute(out_weight, 'tensor', UP)  2.6 us
  transfers between devices with their start and end apart: 2, of which 2 were waited for; matrix products, arithmetic and copies ran while one was open for 0% of the time, Pallas kernels for 4%

profile of v6, /device:TPU:1, one launch (start us, length us, event | category | flops | bytes accessed | tf_op | source)
XLA Modules:
  0.0 70.3 jit_solution(13902181698349694828)
XLA Ops:
  0.0 0.0 copy-start.2
  0.0 2.6 %collective-permute-start = (bf16[512,4096]{1,0:T(8,128)(2,1)}, bf16[512,4096]{1,0:T(8,128)(2,1)S(1)}, u32[]{:S(2)}, u32[]{:S(2)}) collective-permute-start(bf16[512,4096]{1,0:T(8,128)(2,1)} %weight_ref.1), channel_id=1, source_target_pairs={{0,1},{1,2},{2,3},{3,4},{4,5},{5,6},{6,7},{7,0},{8,9},{9,10},{10,1... | collective-permute-start | bytes 12582920 | tf_op jit(solution)/shard_map/ppermute | solution.py:140
  2.6 4.3 %collective-permute-start.1 = (bf16[512,4096]{1,0:T(8,128)(2,1)}, bf16[512,4096]{1,0:T(8,128)(2,1)S(1)}, u32[]{:S(2)}, u32[]{:S(2)}) collective-permute-start(bf16[512,4096]{1,0:T(8,128)(2,1)} %weight_ref.1), channel_id=1, source_target_pairs={{0,7},{1,0},{2,1},{3,2},{4,3},{5,4},{6,5},{7,6},{8,15},{9,8},{10,9... | collective-permute-start | bytes 12582920 | tf_op jit(solution)/shard_map/ppermute | solution.py:141
  6.9 1.6 %shard_map.64 = (f32[4,128,128]{2,1,0:T(8,128)S(1)}, f32[16,8,512]{2,1,0:T(8,128)S(1)}, bf16[8,16,512]{2,1,0:T(8,128)(2,1)S(1)}) custom-call(bf16[128,512]{1,0:T(8,128)(2,1)} %gate_hbm.1, bf16[128,512]{1,0:T(8,128)(2,1)} %value_hbm.1, f32[16,512]{1,0:T(8,128)} %rate_ref.3), custom_call_target="tpu_custom_call" | custom-call | flops 8000000000 | bytes 1000000 | tf_op jit(solution)/shard_map/pallas_call | solution.py:143
  8.5 10.3 %all_to_all.15.came_ref = bf16[8,16,512]{2,1,0:T(8,128)(2,1)S(1)} all-to-all(bf16[8,16,512]{2,1,0:T(8,128)(2,1)S(1)} %get-tuple-element.8), channel_id=1, replica_groups={{0,64,128,192,256,320,384,448},{8,72,136,200,264,328,392,456},{16,80,14..., dimensions={0} | all-to-all | bytes 262144 | tf_op jit(solution)/shard_map/all_to_all | solution.py:155
  18.8 0.0 copy-done.2
  18.8 0.0 copy-start.1
  18.8 0.0 copy-start.3
  18.8 0.0 copy-start
  18.8 0.1 shard_map.65
  18.9 18.2 %all_to_all.16.came_ref = bf16[8,16,512]{2,1,0:T(8,128)(2,1)S(1)} all-to-all(bf16[8,16,512]{2,1,0:T(8,128)(2,1)S(1)} %shard_map.65), channel_id=1, replica_groups={{0,8,16,24,32,40,48,56},{64,72,80,88,96,104,112,120},{128,136,144,152,1..., dimensions={0} | all-to-all | bytes 262144 | tf_op jit(solution)/shard_map/all_to_all | solution.py:159
  37.0 0.0 copy-done.1
  37.0 0.0 copy-done.3
  37.0 1.0 %shard_map.66 = bf16[128,512]{1,0:T(8,128)(2,1)S(1)} custom-call(bf16[8,16,512]{2,1,0:T(8,128)(2,1)S(1)} %all_to_all.16.came_ref, f32[16,8,512]{2,1,0:T(8,128)S(1)} %get-tuple-element.9.ends_ref, f32[4,128,128]{2,1,0:T(8,128)S(1)} %get-tuple-element.10.x_ref, bf16[128,512]{1,0:T(8,128)(2,1)S(1)} %copy-done.1, f32[16,512]{1,0:T(8,128)S(1)} %copy-done.3, ...), custom_call_target="tpu_custom_call" | custom-call | flops 100000 | bytes 10000 | tf_op jit(solution)/shard_map/pallas_call | solution.py:161
  38.0 6.1 %all-gather = bf16[256,512]{1,0:T(8,128)(2,1)S(1)} all-gather(bf16[128,512]{1,0:T(8,128)(2,1)S(1)} %shard_map.66), channel_id=2, replica_groups={{0,1},{2,3},{4,5},{6,7},{8,9},{10,11},{12,13},{14,15},{16,17},{18,19},{..., dimensions={0}, use_global_device_ids=true | all-gather | bytes 393216 | tf_op jit(solution)/shard_map/all_gather | solution.py:167
  44.2 4.2 %collective-permute-done.up_ref = bf16[512,4096]{1,0:T(8,128)(2,1)S(1)} collective-permute-done((bf16[512,4096]{1,0:T(8,128)(2,1)}, bf16[512,4096]{1,0:T(8,128)(2,1)S(1)}, u32[]{:S(2)}, u32[]{:S(2)}) %collective-permute-start) | collective-permute-done | bytes 4194336 | tf_op jit(solution)/shard_map/ppermute | solution.py:140
  48.4 2.7 %collective-permute-done.1.down_ref = bf16[512,4096]{1,0:T(8,128)(2,1)S(1)} collective-permute-done((bf16[512,4096]{1,0:T(8,128)(2,1)}, bf16[512,4096]{1,0:T(8,128)(2,1)S(1)}, u32[]{:S(2)}, u32[]{:S(2)}) %collective-permute-start.1) | collective-permute-done | bytes 4194336 | tf_op jit(solution)/shard_map/ppermute | solution.py:141
  51.0 0.0 copy-done
  51.0 0.7 %shard_map.67 = bf16[4,128,512]{2,1,0:T(8,128)(2,1)S(1)} custom-call(bf16[2,128,512]{2,1,0:T(8,128)(2,1)S(1)} %bitcast.1, bf16[512,4096]{1,0:T(8,128)(2,1)S(1)} %copy-done, bf16[512,4096]{1,0:T(8,128)(2,1)S(1)} %collective-permute-done.up_ref, bf16[512,4096]{1,0:T(8,128)(2,1)S(1)} %collective-permute-done.1.down_ref), custom_call_target="tpu_custom_call" | custom-call | flops 600000000 | bytes 5000000 | tf_op jit(solution)/shard_map/pallas_call | solution.py:168
  51.8 17.8 %all_to_all.17.came_ref = bf16[4,128,512]{2,1,0:T(8,128)(2,1)S(1)} all-to-all(bf16[4,128,512]{2,1,0:T(8,128)(2,1)S(1)} %shard_map.67), channel_id=1, replica_groups={{0,2,4,6},{1,3,5,7},{8,10,12,14},{9,11,13,15},{16,18,20,22},{17,19,21,2..., dimensions={0} | all-to-all | bytes 1048576 | tf_op jit(solution)/shard_map/all_to_all | solution.py:171
  69.6 0.7 %shard_map.68 = bf16[128,512]{1,0:T(8,128)(2,1)} custom-call(bf16[4,128,512]{2,1,0:T(8,128)(2,1)S(1)} %all_to_all.17.came_ref), custom_call_target="tpu_custom_call" | custom-call | flops 300000 | bytes 700000 | tf_op jit(solution)/shard_map/pallas_call | solution.py:172
Async XLA Ops:
  0.0 18.8 %copy-start.2 = (f32[16,512]{1,0:T(8,128)S(1)}, f32[16,512]{1,0:T(8,128)}, u32[]{:S(2)}) copy-start(f32[16,512]{1,0:T(8,128)} %rate_ref.3) | copy-start | bytes 98308
  0.0 48.4 %collective-permute-start = (bf16[512,4096]{1,0:T(8,128)(2,1)}, bf16[512,4096]{1,0:T(8,128)(2,1)S(1)}, u32[]{:S(2)}, u32[]{:S(2)}) collective-permute-start(bf16[512,4096]{1,0:T(8,128)(2,1)} %weight_ref.1), channel_id=1, source_target_pairs={{0,1},{1,2},{2,3},{3,4},{4,5},{5,6},{6,7},{7,0},{8,9},{9,10},{10,1... | collective-permute-start | bytes 12582920 | tf_op jit(solution)/shard_map/ppermute | solution.py:140
  2.6 48.4 %collective-permute-start.1 = (bf16[512,4096]{1,0:T(8,128)(2,1)}, bf16[512,4096]{1,0:T(8,128)(2,1)S(1)}, u32[]{:S(2)}, u32[]{:S(2)}) collective-permute-start(bf16[512,4096]{1,0:T(8,128)(2,1)} %weight_ref.1), channel_id=1, source_target_pairs={{0,7},{1,0},{2,1},{3,2},{4,3},{5,4},{6,5},{7,6},{8,15},{9,8},{10,9... | collective-permute-start | bytes 12582920 | tf_op jit(solution)/shard_map/ppermute | solution.py:141
  18.8 18.3 %copy-start.1 = (bf16[128,512]{1,0:T(8,128)(2,1)S(1)}, bf16[128,512]{1,0:T(8,128)(2,1)}, u32[]{:S(2)}) copy-start(bf16[128,512]{1,0:T(8,128)(2,1)} %query_ref.1) | copy-start | bytes 393220
  18.8 18.3 %copy-start.3 = (f32[16,512]{1,0:T(8,128)S(1)}, f32[16,512]{1,0:T(8,128)}, u32[]{:S(2)}) copy-start(f32[16,512]{1,0:T(8,128)} %residue_ref.1) | copy-start | bytes 98308
  18.8 32.2 %copy-start = (bf16[512,4096]{1,0:T(8,128)(2,1)S(1)}, bf16[512,4096]{1,0:T(8,128)(2,1)}, u32[]{:S(2)}) copy-start(bf16[512,4096]{1,0:T(8,128)(2,1)} %weight_ref.1) | copy-start | bytes 12582916

commit v7 on v4

--- a/solution.py
+++ b/solution.py
@@ -17,9 +17,11 @@
 LINK = jnp.bfloat16
 
 GROUPS = tuple(slice(g * LANES, (g + 1) * LANES) for g in range(CHANNELS // LANES))
-Z_GROUPS = [[y * RING + z for z in range(RING)] for y in range(RING)]
-Y_GROUPS = [[y * RING + z for y in range(RING)] for z in range(RING)]
-X_GROUPS = [[x * 2 + core for x in range(XCHIPS)] for core in range(2)]
+ORDER = (0, 4, 2, 6, 1, 5, 3, 7)
+X_ORDER = (0, 2, 1, 3)
+Z_GROUPS = [[y * RING + z for z in ORDER] for y in range(RING)]
+Y_GROUPS = [[y * RING + z for y in ORDER] for z in range(RING)]
+X_GROUPS = [[x * 2 + core for x in X_ORDER] for core in range(2)]
 SIBLING = [(t, t ^ 1) for t in range(2 * XCHIPS)]
 
 
@@ -57,17 +59,22 @@
             send_ref[j, :, lanes] = total
 
 
+def place_of(chip):
+    return 4 * lax.rem(chip, 2) + 2 * lax.rem(chip // 2, 2) + chip // 4
+
+
 def row_carry(came_ref, rate_ref, send_ref):
     context = lax.axis_index("context")
     z, y = lax.rem(context, RING), context // RING
     shrink = jnp.exp(-rate_ref[...] * (RING * ROWS / SEQ))
     prior = jnp.zeros((POLES, CHANNELS), jnp.float32)
     for j in range(RING):
-        prior = jnp.where(j < y, prior * shrink + came_ref[j].astype(jnp.float32), prior)
+        came = came_ref[ORDER[j]].astype(jnp.float32)
+        prior = jnp.where(j < y, prior * shrink + came, prior)
     alone = prior.astype(LINK)
-    both = (prior * shrink + came_ref[y].astype(jnp.float32)).astype(LINK)
+    both = (prior * shrink + came_ref[place_of(y)].astype(jnp.float32)).astype(LINK)
     for j in range(RING):
-        send_ref[j] = jnp.where(j > z, both, alone)
+        send_ref[ORDER[j]] = jnp.where(j > z, both, alone)
 
 
 def convolve_project(
@@ -79,7 +86,8 @@
     shrink = jnp.exp(-rate_ref[...] * (ROWS / SEQ))
     carry = jnp.zeros((POLES, CHANNELS), jnp.float32)
     for j in range(RING):
-        carry = carry * shrink + came_ref[lax.rem(z + j, RING)].astype(jnp.float32)
+        came = came_ref[place_of(lax.rem(z + j, RING))].astype(jnp.float32)
+        carry = carry * shrink + came
     for g, lanes in enumerate(GROUPS):
         rate = rate_ref[:, lanes] / SEQ
         steps = over_subs(rate)
@@ -102,12 +110,12 @@
 
 
 def project(gated, weight_ref, core, out_ref):
-    for chip in range(XCHIPS):
+    for place, chip in enumerate(X_ORDER):
         column = pl.multiple_of((2 * chip + core) * CHANNELS, CHANNELS)
         partial = jnp.dot(
             gated, weight_ref[:, pl.ds(column, CHANNELS)], preferred_element_type=jnp.float32
         )
-        out_ref[chip] = partial.astype(out_ref.dtype)
+        out_ref[place] = partial.astype(out_ref.dtype)
 
 
 def project_own(gated_ref, weight_ref, keep_ref):

time: 56.9 us -> 54.5 us (0.958)
  blocking collectives: 45.8 us -> 43.2 us
    all_to_all x1, blocking collectives: 18 us -> 16.7 us  [on_device(): came = lax.all_to_all(sent, 'context', 0, 0, axis_index_groups=Z_GROUPS)]
    all_to_all x1, blocking collectives: 15.4 us -> 14.3 us  [on_device(): came = lax.all_to_all(sent, 'context', 0, 0, axis_index_groups=Y_GROUPS)]
where the time goes in v7:
time: 54.5 us; the launch traced here: 54.3 us
  blocking collectives  43.2 us (79%)
  starting transfers between devices  5.73 us (11%)
  Pallas kernels  4.29 us (8%)
  waiting for transfers between devices  1.05 us (2%)
    all_to_all x1, blocking collectives, on_device(): came = lax.all_to_all(sent, 'context', 0, 0, axis_index_groups=Z_GROUPS)  16.7 us
    all_to_all x1, blocking collectives, on_device(): came = lax.all_to_all(sent, 'context', 0, 0, axis_index_groups=Y_GROUPS)  14.3 us
    all_to_all x1, blocking collectives, on_device(): came = lax.all_to_all(pair, 'tensor', 0, 0, axis_index_groups=X_GROUPS)  12.2 us
    ppermute x1, starting transfers between devices, on_device(): came = lax.ppermute(sent, 'tensor', SIBLING)  5.73 us
    pallas_call x1, Pallas kernels, on_device(): kernel(end_states, [((len(GROUPS), ROWS, LANES), f32), ((POLES, SUBS, CHA...  1.57 us
    pallas_call x1, Pallas kernels, on_device(): kernel(convolve_project, [(halves, bf16), (rows, bf16)], scratch=[pltpu.V...  1.38 us
  transfers between devices with their start and end apart: 1, of which 1 were waited for; matrix products, arithmetic and copies ran while one was open for 0% of the time, Pallas kernels for 1%

profile of v7, /device:TPU:1, one launch (start us, length us, event | category | flops | bytes accessed | tf_op | source)
XLA Modules:
  0.0 54.3 jit_solution(6560345318936920035)
XLA Ops:
  0.0 0.0 copy-start.2
  0.0 1.6 %shard_map.64 = (f32[4,128,128]{2,1,0:T(8,128)S(1)}, f32[16,8,512]{2,1,0:T(8,128)S(1)}, bf16[8,16,512]{2,1,0:T(8,128)(2,1)S(1)}) custom-call(bf16[128,512]{1,0:T(8,128)(2,1)} %gate_hbm.1, bf16[128,512]{1,0:T(8,128)(2,1)} %value_hbm.1, f32[16,512]{1,0:T(8,128)} %rate_ref.3), custom_call_target="tpu_custom_call" | custom-call | flops 8000000000 | bytes 1000000 | tf_op jit(solution)/shard_map/pallas_call | solution.py:152
  1.6 14.3 %all_to_all.15.came_ref = bf16[8,16,512]{2,1,0:T(8,128)(2,1)S(1)} all-to-all(bf16[8,16,512]{2,1,0:T(8,128)(2,1)S(1)} %get-tuple-element.10), channel_id=1, replica_groups={{0,256,128,384,64,320,192,448},{8,264,136,392,72,328,200,456},{16,272,1..., dimensions={0} | all-to-all | bytes 262144 | tf_op jit(solution)/shard_map/all_to_all | solution.py:164
  15.8 0.0 copy-done.2
  15.8 0.0 copy-start
  15.8 0.0 copy-start.1
  15.8 0.0 copy-start.3
  15.8 0.1 shard_map.65
  15.9 16.7 %all_to_all.16.came_ref = bf16[8,16,512]{2,1,0:T(8,128)(2,1)S(1)} all-to-all(bf16[8,16,512]{2,1,0:T(8,128)(2,1)S(1)} %shard_map.65), channel_id=1, replica_groups={{0,32,16,48,8,40,24,56},{64,96,80,112,72,104,88,120},{128,160,144,176,1..., dimensions={0} | all-to-all | bytes 262144 | tf_op jit(solution)/shard_map/all_to_all | solution.py:168
  32.6 0.0 copy-done
  32.7 0.0 copy-done.1
  32.7 0.0 copy-done.3
  32.7 1.4 %shard_map.66 = (bf16[4,128,512]{2,1,0:T(8,128)(2,1)S(1)}, bf16[128,512]{1,0:T(8,128)(2,1)S(1)}) custom-call(bf16[8,16,512]{2,1,0:T(8,128)(2,1)S(1)} %all_to_all.16.came_ref, f32[16,8,512]{2,1,0:T(8,128)S(1)} %get-tuple-element.11.ends_ref, f32[4,128,128]{2,1,0:T(8,128)S(1)} %get-tuple-element.12.x_ref, bf16[128,512]{1,0:T(8,128)(2,1)S(1)} %copy-done.1, ...), custom_call_target="tpu_custom_call" | custom-call | flops 300000000 | bytes 3000000 | tf_op jit(solution)/shard_map/pallas_call | solution.py:170
  34.0 5.7 %collective-permute-start = (bf16[4,128,512]{2,1,0:T(8,128)(2,1)S(1)}, bf16[4,128,512]{2,1,0:T(8,128)(2,1)S(1)}, u32[]{:S(2)}, u32[]{:S(2)}) collective-permute-start(bf16[4,128,512]{2,1,0:T(8,128)(2,1)S(1)} %get-tuple-element.14), channel_id=1, source_target_pairs={{0,1},{1,0},{2,3},{3,2},{4,5},{5,4},{6,7},{7,6},{8,9},{9,8},{10,11... | collective-permute-start | bytes 1572872 | tf_op jit(solution)/shard_map/ppermute | solution.py:176
  39.8 0.5 shard_map.67.kept_ref
  40.3 1.0 %collective-permute-done.came_ref = bf16[4,128,512]{2,1,0:T(8,128)(2,1)S(1)} collective-permute-done((bf16[4,128,512]{2,1,0:T(8,128)(2,1)S(1)}, bf16[4,128,512]{2,1,0:T(8,128)(2,1)S(1)}, u32[]{:S(2)}, u32[]{:S(2)}) %collective-permute-start) | collective-permute-done | bytes 524320 | tf_op jit(solution)/shard_map/ppermute | solution.py:176
  41.3 0.1 shard_map.68
  41.4 12.2 %all_to_all.17.came_ref = bf16[4,128,512]{2,1,0:T(8,128)(2,1)S(1)} all-to-all(bf16[4,128,512]{2,1,0:T(8,128)(2,1)S(1)} %shard_map.68), channel_id=1, replica_groups={{0,4,2,6},{1,5,3,7},{8,12,10,14},{9,13,11,15},{16,20,18,22},{17,21,19,2..., dimensions={0} | all-to-all | bytes 1048576 | tf_op jit(solution)/shard_map/all_to_all | solution.py:181
  53.6 0.7 %shard_map.69 = bf16[128,512]{1,0:T(8,128)(2,1)} custom-call(bf16[4,128,512]{2,1,0:T(8,128)(2,1)S(1)} %all_to_all.17.came_ref), custom_call_target="tpu_custom_call" | custom-call | flops 300000 | bytes 700000 | tf_op jit(solution)/shard_map/pallas_call | solution.py:182
Async XLA Ops:
  0.0 15.8 %copy-start.2 = (f32[16,512]{1,0:T(8,128)S(1)}, f32[16,512]{1,0:T(8,128)}, u32[]{:S(2)}) copy-start(f32[16,512]{1,0:T(8,128)} %rate_ref.3) | copy-start | bytes 98308
  15.8 16.8 %copy-start = (bf16[512,4096]{1,0:T(8,128)(2,1)S(1)}, bf16[512,4096]{1,0:T(8,128)(2,1)}, u32[]{:S(2)}) copy-start(bf16[512,4096]{1,0:T(8,128)(2,1)} %weight_ref.3) | copy-start | bytes 12582916
  15.8 16.8 %copy-start.1 = (bf16[128,512]{1,0:T(8,128)(2,1)S(1)}, bf16[128,512]{1,0:T(8,128)(2,1)}, u32[]{:S(2)}) copy-start(bf16[128,512]{1,0:T(8,128)(2,1)} %query_ref.1) | copy-start | bytes 393220
  15.8 16.8 %copy-start.3 = (f32[16,512]{1,0:T(8,128)S(1)}, f32[16,512]{1,0:T(8,128)}, u32[]{:S(2)}) copy-start(f32[16,512]{1,0:T(8,128)} %residue_ref.1) | copy-start | bytes 98308
  34.0 7.3 %collective-permute-start = (bf16[4,128,512]{2,1,0:T(8,128)(2,1)S(1)}, bf16[4,128,512]{2,1,0:T(8,128)(2,1)S(1)}, u32[]{:S(2)}, u32[]{:S(2)}) collective-permute-start(bf16[4,128,512]{2,1,0:T(8,128)(2,1)S(1)} %get-tuple-element.14), channel_id=1, source_target_pairs={{0,1},{1,0},{2,3},{3,2},{4,5},{5,4},{6,7},{7,6},{8,9},{9,8},{10,11... | collective-permute-start | bytes 1572872 | tf_op jit(solution)/shard_map/ppermute | solution.py:176

commit v8 on v7

--- a/solution.py
+++ b/solution.py
@@ -17,10 +17,11 @@
 LINK = jnp.bfloat16
 
 GROUPS = tuple(slice(g * LANES, (g + 1) * LANES) for g in range(CHANNELS // LANES))
-ORDER = (0, 4, 2, 6, 1, 5, 3, 7)
-X_ORDER = (0, 2, 1, 3)
-Z_GROUPS = [[y * RING + z for z in ORDER] for y in range(RING)]
-Y_GROUPS = [[y * RING + z for y in ORDER] for z in range(RING)]
+Y_ORDER = (4, 0, 6, 2, 5, 1, 7, 3)
+Z_ORDER = (4, 0, 6, 2, 5, 1, 7, 3)
+X_ORDER = (3, 1, 2, 0)
+Z_GROUPS = [[y * RING + z for z in Z_ORDER] for y in range(RING)]
+Y_GROUPS = [[y * RING + z for y in Y_ORDER] for z in range(RING)]
 X_GROUPS = [[x * 2 + core for x in X_ORDER] for core in range(2)]
 SIBLING = [(t, t ^ 1) for t in range(2 * XCHIPS)]
 
@@ -59,8 +60,11 @@
             send_ref[j, :, lanes] = total
 
 
-def place_of(chip):
-    return 4 * lax.rem(chip, 2) + 2 * lax.rem(chip // 2, 2) + chip // 4
+def place_of(chip, order):
+    place = 0
+    for index in range(1, RING):
+        place = jnp.where(chip == order[index], index, place)
+    return place
 
 
 def row_carry(came_ref, rate_ref, send_ref):
@@ -69,12 +73,12 @@
     shrink = jnp.exp(-rate_ref[...] * (RING * ROWS / SEQ))
     prior = jnp.zeros((POLES, CHANNELS), jnp.float32)
     for j in range(RING):
-        came = came_ref[ORDER[j]].astype(jnp.float32)
+        came = came_ref[Y_ORDER.index(j)].astype(jnp.float32)
         prior = jnp.where(j < y, prior * shrink + came, prior)
     alone = prior.astype(LINK)
-    both = (prior * shrink + came_ref[place_of(y)].astype(jnp.float32)).astype(LINK)
+    both = (prior * shrink + came_ref[place_of(y, Y_ORDER)].astype(jnp.float32)).astype(LINK)
     for j in range(RING):
-        send_ref[ORDER[j]] = jnp.where(j > z, both, alone)
+        send_ref[Z_ORDER.index(j)] = jnp.where(j > z, both, alone)
 
 
 def convolve_project(
@@ -86,7 +90,7 @@
     shrink = jnp.exp(-rate_ref[...] * (ROWS / SEQ))
     carry = jnp.zeros((POLES, CHANNELS), jnp.float32)
     for j in range(RING):
-        came = came_ref[place_of(lax.rem(z + j, RING))].astype(jnp.float32)
+        came = came_ref[place_of(lax.rem(z + j, RING), Z_ORDER)].astype(jnp.float32)
         carry = carry * shrink + came
     for g, lanes in enumerate(GROUPS):
         rate = rate_ref[:, lanes] / SEQ

time: 54.5 us -> 50.2 us (0.921)
  blocking collectives: 43.2 us -> 40.2 us
  starting transfers between devices: 5.73 us -> 4.32 us
    all_to_all x1, blocking collectives: 14.3 us -> 11.6 us  [on_device(): came = lax.all_to_all(sent, 'context', 0, 0, axis_index_groups=Y_GROUPS)]
    ppermute x1, starting transfers between devices: 5.73 us -> 4.32 us  [on_device(): came = lax.ppermute(sent, 'tensor', SIBLING)]
    all_to_all x1, blocking collectives: 12.2 us -> 11.6 us  [on_device(): came = lax.all_to_all(pair, 'tensor', 0, 0, axis_index_groups=X_GROUPS)]
where the time goes in v8:
time: 50.2 us; the launch traced here: 49.9 us
  blocking collectives  40.2 us (80%)
  starting transfers between devices  4.32 us (9%)
  Pallas kernels  4.27 us (9%)
  waiting for transfers between devices  1.04 us (2%)
    all_to_all x1, blocking collectives, on_device(): came = lax.all_to_all(sent, 'context', 0, 0, axis_index_groups=Z_GROUPS)  17 us
    all_to_all x1, blocking collectives, on_device(): came = lax.all_to_all(pair, 'tensor', 0, 0, axis_index_groups=X_GROUPS)  11.6 us
    all_to_all x1, blocking collectives, on_device(): came = lax.all_to_all(sent, 'context', 0, 0, axis_index_groups=Y_GROUPS)  11.6 us
    ppermute x1, starting transfers between devices, on_device(): came = lax.ppermute(sent, 'tensor', SIBLING)  4.32 us
    pallas_call x1, Pallas kernels, on_device(): kernel(end_states, [((len(GROUPS), ROWS, LANES), f32), ((POLES, SUBS, CHA...  1.57 us
    pallas_call x1, Pallas kernels, on_device(): kernel(convolve_project, [(halves, bf16), (rows, bf16)], scratch=[pltpu.V...  1.35 us
    ppermute x1, waiting for transfers between devices, on_device(): came = lax.ppermute(sent, 'tensor', SIBLING)  1.04 us
  transfers between devices with their start and end apart: 1, of which 1 were waited for; matrix products, arithmetic and copies ran while one was open for 0% of the time, Pallas kernels for 1%

profile of v8, /device:TPU:1, one launch (start us, length us, event | category | flops | bytes accessed | tf_op | source)
XLA Modules:
  0.0 49.9 jit_solution(7779027652252695934)
XLA Ops:
  0.0 0.0 copy-start.2
  0.0 1.6 %shard_map.64 = (f32[4,128,128]{2,1,0:T(8,128)S(1)}, f32[16,8,512]{2,1,0:T(8,128)S(1)}, bf16[8,16,512]{2,1,0:T(8,128)(2,1)S(1)}) custom-call(bf16[128,512]{1,0:T(8,128)(2,1)} %gate_hbm.1, bf16[128,512]{1,0:T(8,128)(2,1)} %value_hbm.1, f32[16,512]{1,0:T(8,128)} %rate_ref.3), custom_call_target="tpu_custom_call" | custom-call | flops 8000000000 | bytes 1000000 | tf_op jit(solution)/shard_map/pallas_call | solution.py:156
  1.6 11.6 %all_to_all.15.came_ref = bf16[8,16,512]{2,1,0:T(8,128)(2,1)S(1)} all-to-all(bf16[8,16,512]{2,1,0:T(8,128)(2,1)S(1)} %get-tuple-element.10), channel_id=1, replica_groups={{256,0,384,128,320,64,448,192},{264,8,392,136,328,72,456,200},{272,16,4..., dimensions={0} | all-to-all | bytes 262144 | tf_op jit(solution)/shard_map/all_to_all | solution.py:168
  13.2 0.0 copy-done.2
  13.2 0.0 copy-start
  13.2 0.0 copy-start.1
  13.2 0.0 copy-start.3
  13.2 0.1 shard_map.65
  13.3 17.0 %all_to_all.16.came_ref = bf16[8,16,512]{2,1,0:T(8,128)(2,1)S(1)} all-to-all(bf16[8,16,512]{2,1,0:T(8,128)(2,1)S(1)} %shard_map.65), channel_id=1, replica_groups={{32,0,48,16,40,8,56,24},{96,64,112,80,104,72,120,88},{160,128,176,144,1..., dimensions={0} | all-to-all | bytes 262144 | tf_op jit(solution)/shard_map/all_to_all | solution.py:172
  30.3 0.0 copy-done
  30.3 0.0 copy-done.1
  30.3 0.0 copy-done.3
  30.3 1.4 %shard_map.66 = (bf16[4,128,512]{2,1,0:T(8,128)(2,1)S(1)}, bf16[128,512]{1,0:T(8,128)(2,1)S(1)}) custom-call(bf16[8,16,512]{2,1,0:T(8,128)(2,1)S(1)} %all_to_all.16.came_ref, f32[16,8,512]{2,1,0:T(8,128)S(1)} %get-tuple-element.11.ends_ref, f32[4,128,128]{2,1,0:T(8,128)S(1)} %get-tuple-element.12.x_ref, bf16[128,512]{1,0:T(8,128)(2,1)S(1)} %copy-done.1, ...), custom_call_target="tpu_custom_call" | custom-call | flops 300000000 | bytes 3000000 | tf_op jit(solution)/shard_map/pallas_call | solution.py:174
  31.7 4.3 %collective-permute-start = (bf16[4,128,512]{2,1,0:T(8,128)(2,1)S(1)}, bf16[4,128,512]{2,1,0:T(8,128)(2,1)S(1)}, u32[]{:S(2)}, u32[]{:S(2)}) collective-permute-start(bf16[4,128,512]{2,1,0:T(8,128)(2,1)S(1)} %get-tuple-element.14), channel_id=1, source_target_pairs={{0,1},{1,0},{2,3},{3,2},{4,5},{5,4},{6,7},{7,6},{8,9},{9,8},{10,11... | collective-permute-start | bytes 1572872 | tf_op jit(solution)/shard_map/ppermute | solution.py:180
  36.0 0.5 shard_map.67.kept_ref
  36.5 1.0 %collective-permute-done.came_ref = bf16[4,128,512]{2,1,0:T(8,128)(2,1)S(1)} collective-permute-done((bf16[4,128,512]{2,1,0:T(8,128)(2,1)S(1)}, bf16[4,128,512]{2,1,0:T(8,128)(2,1)S(1)}, u32[]{:S(2)}, u32[]{:S(2)}) %collective-permute-start) | collective-permute-done | bytes 524320 | tf_op jit(solution)/shard_map/ppermute | solution.py:180
  37.5 0.1 shard_map.68
  37.6 11.6 %all_to_all.17.came_ref = bf16[4,128,512]{2,1,0:T(8,128)(2,1)S(1)} all-to-all(bf16[4,128,512]{2,1,0:T(8,128)(2,1)S(1)} %shard_map.68), channel_id=1, replica_groups={{6,2,4,0},{7,3,5,1},{14,10,12,8},{15,11,13,9},{22,18,20,16},{23,19,21,1..., dimensions={0} | all-to-all | bytes 1048576 | tf_op jit(solution)/shard_map/all_to_all | solution.py:185
  49.2 0.7 %shard_map.69 = bf16[128,512]{1,0:T(8,128)(2,1)} custom-call(bf16[4,128,512]{2,1,0:T(8,128)(2,1)S(1)} %all_to_all.17.came_ref), custom_call_target="tpu_custom_call" | custom-call | flops 300000 | bytes 700000 | tf_op jit(solution)/shard_map/pallas_call | solution.py:186
Async XLA Ops:
  0.0 13.2 %copy-start.2 = (f32[16,512]{1,0:T(8,128)S(1)}, f32[16,512]{1,0:T(8,128)}, u32[]{:S(2)}) copy-start(f32[16,512]{1,0:T(8,128)} %rate_ref.3) | copy-start | bytes 98308
  13.2 17.1 %copy-start = (bf16[512,4096]{1,0:T(8,128)(2,1)S(1)}, bf16[512,4096]{1,0:T(8,128)(2,1)}, u32[]{:S(2)}) copy-start(bf16[512,4096]{1,0:T(8,128)(2,1)} %weight_ref.3) | copy-start | bytes 12582916
  13.2 17.1 %copy-start.1 = (bf16[128,512]{1,0:T(8,128)(2,1)S(1)}, bf16[128,512]{1,0:T(8,128)(2,1)}, u32[]{:S(2)}) copy-start(bf16[128,512]{1,0:T(8,128)(2,1)} %query_ref.1) | copy-start | bytes 393220
  13.2 17.1 %copy-start.3 = (f32[16,512]{1,0:T(8,128)S(1)}, f32[16,512]{1,0:T(8,128)}, u32[]{:S(2)}) copy-start(f32[16,512]{1,0:T(8,128)} %residue_ref.1) | copy-start | bytes 98308
  31.7 5.8 %collective-permute-start = (bf16[4,128,512]{2,1,0:T(8,128)(2,1)S(1)}, bf16[4,128,512]{2,1,0:T(8,128)(2,1)S(1)}, u32[]{:S(2)}, u32[]{:S(2)}) collective-permute-start(bf16[4,128,512]{2,1,0:T(8,128)(2,1)S(1)} %get-tuple-element.14), channel_id=1, source_target_pairs={{0,1},{1,0},{2,3},{3,2},{4,5},{5,4},{6,7},{7,6},{8,9},{9,8},{10,11... | collective-permute-start | bytes 1572872 | tf_op jit(solution)/shard_map/ppermute | solution.py:180

commit v9 on v2

--- a/solution.py
+++ b/solution.py
@@ -17,9 +17,12 @@
 LINK = jnp.bfloat16
 
 GROUPS = tuple(slice(g * LANES, (g + 1) * LANES) for g in range(CHANNELS // LANES))
-Z_GROUPS = [[y * RING + z for z in range(RING)] for y in range(RING)]
-Y_GROUPS = [[y * RING + z for y in range(RING)] for z in range(RING)]
-X_GROUPS = [[x * 2 + core for x in range(XCHIPS)] for core in range(2)]
+Y_ORDER = (4, 0, 6, 2, 5, 1, 7, 3)
+Z_ORDER = (7, 3, 5, 1, 6, 2, 4, 0)
+X_ORDER = (3, 1, 2, 0)
+Z_GROUPS = [[y * RING + z for z in Z_ORDER] for y in range(RING)]
+Y_GROUPS = [[y * RING + z for y in Y_ORDER] for z in range(RING)]
+X_GROUPS = [[x * 2 + core for x in X_ORDER] for core in range(2)]
 SIBLING = [(t, t ^ 1) for t in range(2 * XCHIPS)]
 
 
@@ -63,7 +66,7 @@
     prior = jnp.zeros((POLES, CHANNELS), jnp.float32)
     total = jnp.zeros((POLES, CHANNELS), jnp.float32)
     for j in range(RING):
-        came = came_ref[j].astype(jnp.float32)
+        came = came_ref[Z_ORDER.index(j)].astype(jnp.float32)
         prior = jnp.where(j < z, prior * shrink + came, prior)
         total = total * shrink + came
     prior_ref[...] = prior
@@ -82,7 +85,7 @@
     shrink = jnp.exp(-rate_ref[...] * (RING * ROWS / SEQ))
     carry = jnp.zeros((POLES, CHANNELS), jnp.float32)
     for j in range(RING):
-        carry = jnp.where(j < y, carry * shrink + came_ref[j].astype(jnp.float32), carry)
+        carry = jnp.where(j < y, carry * shrink + came_ref[Y_ORDER.index(j)].astype(jnp.float32), carry)
     behind = (z * ROWS).astype(jnp.float32) / SEQ
     carry = carry * jnp.exp(-rate_ref[...] * behind) + prior_ref[...]
     for g, lanes in enumerate(GROUPS):
@@ -107,12 +110,12 @@
 
 
 def project(gated, weight_ref, core, out_ref):
-    for chip in range(XCHIPS):
+    for place, chip in enumerate(X_ORDER):
         column = pl.multiple_of((2 * chip + core) * CHANNELS, CHANNELS)
         partial = jnp.dot(
             gated, weight_ref[:, pl.ds(column, CHANNELS)], preferred_element_type=jnp.float32
         )
-        out_ref[chip] = partial.astype(out_ref.dtype)
+        out_ref[place] = partial.astype(out_ref.dtype)
 
 
 def project_own(gated_ref, weight_ref, keep_ref):

time: 56.9 us -> 49.9 us (0.88)
  blocking collectives: 45.8 us -> 39.6 us
  starting transfers between devices: 5.54 us -> 4.67 us
    all_to_all x1, blocking collectives: 14.9 us -> 11.3 us  [on_device(): came = lax.all_to_all(sent, 'context', 0, 0, axis_index_groups=Y_GROUPS)]
    all_to_all x1, blocking collectives: 18.4 us -> 16.7 us  [on_device(): came = lax.all_to_all(sent, 'context', 0, 0, axis_index_groups=Z_GROUPS)]
    ppermute x1, starting transfers between devices: 5.54 us -> 4.67 us  [on_device(): came = lax.ppermute(sent, 'tensor', SIBLING)]
    all_to_all x1, blocking collectives: 12.4 us -> 11.6 us  [on_device(): came = lax.all_to_all(pair, 'tensor', 0, 0, axis_index_groups=X_GROUPS)]
where the time goes in v9:
time: 49.9 us; the launch traced here: 49.7 us
  blocking collectives  39.6 us (79%)
  starting transfers between devices  4.67 us (9%)
  Pallas kernels  4.28 us (9%)
  waiting for transfers between devices  1.04 us (2%)
    all_to_all x1, blocking collectives, on_device(): came = lax.all_to_all(sent, 'context', 0, 0, axis_index_groups=Z_GROUPS)  16.7 us
    all_to_all x1, blocking collectives, on_device(): came = lax.all_to_all(pair, 'tensor', 0, 0, axis_index_groups=X_GROUPS)  11.6 us
    all_to_all x1, blocking collectives, on_device(): came = lax.all_to_all(sent, 'context', 0, 0, axis_index_groups=Y_GROUPS)  11.3 us
    ppermute x1, starting transfers between devices, on_device(): came = lax.ppermute(sent, 'tensor', SIBLING)  4.67 us
    pallas_call x1, Pallas kernels, on_device(): kernel(end_states, [((len(GROUPS), ROWS, LANES), f32), ((POLES, SUBS, CHA...  1.57 us
    pallas_call x1, Pallas kernels, on_device(): kernel(convolve_project, [(halves, bf16), (rows, bf16)], scratch=[pltpu.V...  1.37 us
    ppermute x1, waiting for transfers between devices, on_device(): came = lax.ppermute(sent, 'tensor', SIBLING)  1.04 us
  transfers between devices with their start and end apart: 1, of which 1 were waited for; matrix products, arithmetic and copies ran while one was open for 0% of the time, Pallas kernels for 1%

profile of v9, /device:TPU:1, one launch (start us, length us, event | category | flops | bytes accessed | tf_op | source)
XLA Modules:
  0.0 49.7 jit_solution(1139970413114458175)
XLA Ops:
  0.0 0.0 copy-start.2
  0.0 1.6 %shard_map.64 = (f32[4,128,128]{2,1,0:T(8,128)S(1)}, f32[16,8,512]{2,1,0:T(8,128)S(1)}, bf16[8,16,512]{2,1,0:T(8,128)(2,1)S(1)}) custom-call(bf16[128,512]{1,0:T(8,128)(2,1)} %gate_hbm.1, bf16[128,512]{1,0:T(8,128)(2,1)} %value_hbm.1, f32[16,512]{1,0:T(8,128)} %rate_ref.3), custom_call_target="tpu_custom_call" | custom-call | flops 8000000000 | bytes 1000000 | tf_op jit(solution)/shard_map/pallas_call | solution.py:152
  1.6 16.7 %all_to_all.15.came_ref = bf16[8,16,512]{2,1,0:T(8,128)(2,1)S(1)} all-to-all(bf16[8,16,512]{2,1,0:T(8,128)(2,1)S(1)} %get-tuple-element.12), channel_id=1, replica_groups={{56,24,40,8,48,16,32,0},{120,88,104,72,112,80,96,64},{184,152,168,136,1..., dimensions={0} | all-to-all | bytes 262144 | tf_op jit(solution)/shard_map/all_to_all | solution.py:164
  18.3 0.0 copy-done.2
  18.3 0.0 copy-start
  18.3 0.0 copy-start.1
  18.3 0.0 copy-start.3
  18.3 0.1 shard_map.65
  18.4 11.3 %all_to_all.16.came_ref = bf16[8,16,512]{2,1,0:T(8,128)(2,1)S(1)} all-to-all(bf16[8,16,512]{2,1,0:T(8,128)(2,1)S(1)} %get-tuple-element.13), channel_id=1, replica_groups={{256,0,384,128,320,64,448,192},{264,8,392,136,328,72,456,200},{272,16,4..., dimensions={0} | all-to-all | bytes 262144 | tf_op jit(solution)/shard_map/all_to_all | solution.py:168
  29.7 0.0 copy-done
  29.7 0.0 copy-done.1
  29.7 0.0 copy-done.3
  29.7 1.4 %shard_map.66 = (bf16[4,128,512]{2,1,0:T(8,128)(2,1)S(1)}, bf16[128,512]{1,0:T(8,128)(2,1)S(1)}) custom-call(bf16[8,16,512]{2,1,0:T(8,128)(2,1)S(1)} %all_to_all.16.came_ref, f32[16,512]{1,0:T(8,128)S(1)} %get-tuple-element.14.prior_ref, f32[16,8,512]{2,1,0:T(8,128)S(1)} %get-tuple-element.15.ends_ref, f32[4,128,128]{2,1,0:T(8,128)S(1)} %get-tuple-element.16.x_ref, ...), custom_call_target="tpu_custom_call" | custom-call | flops 300000000 | bytes 3000000 | tf_op jit(solution)/shard_map/pallas_call | solution.py:170
  31.1 4.7 %collective-permute-start = (bf16[4,128,512]{2,1,0:T(8,128)(2,1)S(1)}, bf16[4,128,512]{2,1,0:T(8,128)(2,1)S(1)}, u32[]{:S(2)}, u32[]{:S(2)}) collective-permute-start(bf16[4,128,512]{2,1,0:T(8,128)(2,1)S(1)} %get-tuple-element.18), channel_id=1, source_target_pairs={{0,1},{1,0},{2,3},{3,2},{4,5},{5,4},{6,7},{7,6},{8,9},{9,8},{10,11... | collective-permute-start | bytes 1572872 | tf_op jit(solution)/shard_map/ppermute | solution.py:176
  35.8 0.5 shard_map.67.kept_ref
  36.2 1.0 %collective-permute-done.came_ref = bf16[4,128,512]{2,1,0:T(8,128)(2,1)S(1)} collective-permute-done((bf16[4,128,512]{2,1,0:T(8,128)(2,1)S(1)}, bf16[4,128,512]{2,1,0:T(8,128)(2,1)S(1)}, u32[]{:S(2)}, u32[]{:S(2)}) %collective-permute-start) | collective-permute-done | bytes 524320 | tf_op jit(solution)/shard_map/ppermute | solution.py:176
  37.3 0.1 shard_map.68
  37.4 11.6 %all_to_all.17.came_ref = bf16[4,128,512]{2,1,0:T(8,128)(2,1)S(1)} all-to-all(bf16[4,128,512]{2,1,0:T(8,128)(2,1)S(1)} %shard_map.68), channel_id=1, replica_groups={{6,2,4,0},{7,3,5,1},{14,10,12,8},{15,11,13,9},{22,18,20,16},{23,19,21,1..., dimensions={0} | all-to-all | bytes 1048576 | tf_op jit(solution)/shard_map/all_to_all | solution.py:181
  49.0 0.7 %shard_map.69 = bf16[128,512]{1,0:T(8,128)(2,1)} custom-call(bf16[4,128,512]{2,1,0:T(8,128)(2,1)S(1)} %all_to_all.17.came_ref), custom_call_target="tpu_custom_call" | custom-call | flops 300000 | bytes 700000 | tf_op jit(solution)/shard_map/pallas_call | solution.py:182
Async XLA Ops:
  0.0 18.3 %copy-start.2 = (f32[16,512]{1,0:T(8,128)S(1)}, f32[16,512]{1,0:T(8,128)}, u32[]{:S(2)}) copy-start(f32[16,512]{1,0:T(8,128)} %rate_ref.3) | copy-start | bytes 98308
  18.3 11.4 %copy-start = (bf16[512,4096]{1,0:T(8,128)(2,1)S(1)}, bf16[512,4096]{1,0:T(8,128)(2,1)}, u32[]{:S(2)}) copy-start(bf16[512,4096]{1,0:T(8,128)(2,1)} %weight_ref.3) | copy-start | bytes 12582916
  18.3 11.4 %copy-start.1 = (bf16[128,512]{1,0:T(8,128)(2,1)S(1)}, bf16[128,512]{1,0:T(8,128)(2,1)}, u32[]{:S(2)}) copy-start(bf16[128,512]{1,0:T(8,128)(2,1)} %query_ref.1) | copy-start | bytes 393220
  18.3 11.4 %copy-start.3 = (f32[16,512]{1,0:T(8,128)S(1)}, f32[16,512]{1,0:T(8,128)}, u32[]{:S(2)}) copy-start(f32[16,512]{1,0:T(8,128)} %residue_ref.1) | copy-start | bytes 98308
  31.1 6.2 %collective-permute-start = (bf16[4,128,512]{2,1,0:T(8,128)(2,1)S(1)}, bf16[4,128,512]{2,1,0:T(8,128)(2,1)S(1)}, u32[]{:S(2)}, u32[]{:S(2)}) collective-permute-start(bf16[4,128,512]{2,1,0:T(8,128)(2,1)S(1)} %get-tuple-element.18), channel_id=1, source_target_pairs={{0,1},{1,0},{2,3},{3,2},{4,5},{5,4},{6,7},{7,6},{8,9},{9,8},{10,11... | collective-permute-start | bytes 1572872 | tf_op jit(solution)/shard_map/ppermute | solution.py:176

commit v10 on v9

--- a/solution.py
+++ b/solution.py
@@ -30,12 +30,9 @@
     return jnp.broadcast_to(rows[:, None, :], (POLES, SUBS, LANES))
 
 
-def sub_index():
-    return lax.broadcasted_iota(jnp.int32, (POLES, SUBS, LANES), 1).astype(jnp.float32)
-
-
 def end_states(
-    gate_hbm, value_hbm, rate_hbm, x_ref, ends_ref, send_ref, gate_ref, value_ref, rate_ref, sems
+    gate_hbm, value_hbm, rate_hbm, x_ref, before_ref, fade_ref, send_ref,
+    gate_ref, value_ref, rate_ref, sems,
 ):
     pairs = ((gate_hbm, gate_ref), (value_hbm, value_ref), (rate_hbm, rate_ref))
     copies = [pltpu.make_async_copy(a, b, sems.at[i]) for i, (a, b) in enumerate(pairs)]
@@ -53,9 +50,17 @@
         for t in range(STEPS):
             row = x_ref[g, pl.ds(t, SUBS, stride=STEPS), :]
             state = shrink * state + row[None]
-        ends_ref[:, :, lanes] = state
-        left = STEPS * (SUBS - 1.0 - sub_index())
-        total = jnp.sum(state * jnp.exp(-over_subs(rate) * left), axis=1).astype(LINK)
+        shrink = over_subs(jnp.exp(-rate * STEPS))
+        fade = jnp.ones_like(state)
+        sub = lax.broadcasted_iota(jnp.int32, state.shape, 1)
+        for shift in (1, 2, 4):
+            later = sub >= shift
+            state = state + pltpu.roll(state, shift, 1) * jnp.where(later, shrink, 0.0)
+            fade = fade * jnp.where((sub & shift) > 0, shrink, 1.0)
+            shrink = shrink * shrink
+        before_ref[:, :, lanes] = jnp.where(sub > 0, pltpu.roll(state, 1, 1), 0.0)
+        fade_ref[:, :, lanes] = fade
+        total = state[:, SUBS - 1, :].astype(LINK)
         for j in range(RING):
             send_ref[j, :, lanes] = total
 
@@ -76,7 +81,7 @@
 
 
 def convolve_project(
-    came_ref, prior_ref, ends_ref, x_ref, query_ref, residue_ref, rate_ref, weight_ref,
+    came_ref, prior_ref, before_ref, fade_ref, x_ref, query_ref, residue_ref, rate_ref, weight_ref,
     send_ref, gated_ref, y_ref,
 ):
     context = lax.axis_index("context")
@@ -89,15 +94,8 @@
     behind = (z * ROWS).astype(jnp.float32) / SEQ
     carry = carry * jnp.exp(-rate_ref[...] * behind) + prior_ref[...]
     for g, lanes in enumerate(GROUPS):
-        rate = rate_ref[:, lanes] / SEQ
-        steps = over_subs(rate)
-        shrink_sub = jnp.exp(-steps * STEPS)
-        sub = sub_index()
-        state = jnp.where(sub > 0, pltpu.roll(ends_ref[:, :, lanes], 1, 1), over_subs(carry[:, lanes]))
-        for shift in (1, 2, 4):
-            state = state + jnp.where(sub >= shift, pltpu.roll(state, shift, 1), 0.0) * shrink_sub
-            shrink_sub = shrink_sub * shrink_sub
-        shrink_one = over_subs(jnp.exp(-rate))
+        state = before_ref[:, :, lanes] + over_subs(carry[:, lanes]) * fade_ref[:, :, lanes]
+        shrink_one = over_subs(jnp.exp(-rate_ref[:, lanes] / SEQ))
         residue = over_subs(residue_ref[:, lanes])
         for t in range(STEPS):
             row = x_ref[g, pl.ds(t, SUBS, stride=STEPS), :]
@@ -148,10 +146,10 @@
 def on_device(queries, key_gate, values, residues, decay_rates, out_weight):
     f32, bf16 = jnp.float32, jnp.bfloat16
     block = (RING, POLES, CHANNELS)
-    rows, modes = (ROWS, CHANNELS), (POLES, CHANNELS)
-    x, ends, sent = kernel(
+    rows, modes, subs = (ROWS, CHANNELS), (POLES, CHANNELS), (POLES, SUBS, CHANNELS)
+    x, before, fade, sent = kernel(
         end_states,
-        [((len(GROUPS), ROWS, LANES), f32), ((POLES, SUBS, CHANNELS), f32), (block, LINK)],
+        [((len(GROUPS), ROWS, LANES), f32), (subs, f32), (subs, f32), (block, LINK)],
         scratch=[
             pltpu.VMEM(rows, bf16),
             pltpu.VMEM(rows, bf16),
@@ -172,7 +170,7 @@
         [(halves, bf16), (rows, bf16)],
         scratch=[pltpu.VMEM((len(GROUPS), ROWS, LANES), f32)],
         flops=300_000_000, moved=3_000_000,
-    )(came, prior, ends, x, queries, residues, decay_rates, out_weight)
+    )(came, prior, before, fade, x, queries, residues, decay_rates, out_weight)
     came = lax.ppermute(sent, "tensor", SIBLING)
     (kept,) = kernel(project_own, [(halves, f32)], flops=600_000_000, moved=3_000_000)(
         gated, out_weight

time: 49.9 us -> 49.9 us (level)
  no operation moved by 1% of the time
where the time goes in v10:
time: 49.9 us; the launch traced here: 49.6 us
  blocking collectives  39.6 us (79%)
  starting transfers between devices  4.65 us (9%)
  Pallas kernels  4.23 us (8%)
  waiting for transfers between devices  1.05 us (2%)
    all_to_all x1, blocking collectives, on_device(): came = lax.all_to_all(sent, 'context', 0, 0, axis_index_groups=Z_GROUPS)  16.7 us
    all_to_all x1, blocking collectives, on_device(): came = lax.all_to_all(pair, 'tensor', 0, 0, axis_index_groups=X_GROUPS)  11.6 us
    all_to_all x1, blocking collectives, on_device(): came = lax.all_to_all(sent, 'context', 0, 0, axis_index_groups=Y_GROUPS)  11.3 us
    ppermute x1, starting transfers between devices, on_device(): came = lax.ppermute(sent, 'tensor', SIBLING)  4.65 us
    pallas_call x1, Pallas kernels, on_device(): kernel(end_states, [((len(GROUPS), ROWS, LANES), f32), (subs, f32), (subs...  1.68 us
    pallas_call x1, Pallas kernels, on_device(): kernel(convolve_project, [(halves, bf16), (rows, bf16)], scratch=[pltpu.V...  1.21 us
    ppermute x1, waiting for transfers between devices, on_device(): came = lax.ppermute(sent, 'tensor', SIBLING)  1.05 us
  transfers between devices with their start and end apart: 1, of which 1 were waited for; matrix products, arithmetic and copies ran while one was open for 0% of the time, Pallas kernels for 1%

profile of v10, /device:TPU:1, one launch (start us, length us, event | category | flops | bytes accessed | tf_op | source)
XLA Modules:
  0.0 49.6 jit_solution(1436759962298378152)
XLA Ops:
  0.0 0.0 copy-start.2
  0.0 1.7 %shard_map.64 = (f32[4,128,128]{2,1,0:T(8,128)S(1)}, f32[16,8,512]{2,1,0:T(8,128)S(1)}, f32[16,8,512]{2,1,0:T(8,128)S(1)}, bf16[8,16,512]{2,1,0:T(8,128)(2,1)S(1)}) custom-call(bf16[128,512]{1,0:T(8,128)(2,1)} %gate_hbm.1, bf16[128,512]{1,0:T(8,128)(2,1)} %value_hbm.1, f32[16,512]{1,0:T(8,128)} %rate_ref.3), custom_call_target="tpu_custom_call" | custom-call | flops 8000000000 | bytes 1000000 | tf_op jit(solution)/shard_map/pallas_call | solution.py:150
  1.7 16.7 %all_to_all.15.came_ref = bf16[8,16,512]{2,1,0:T(8,128)(2,1)S(1)} all-to-all(bf16[8,16,512]{2,1,0:T(8,128)(2,1)S(1)} %get-tuple-element.13), channel_id=1, replica_groups={{56,24,40,8,48,16,32,0},{120,88,104,72,112,80,96,64},{184,152,168,136,1..., dimensions={0} | all-to-all | bytes 262144 | tf_op jit(solution)/shard_map/all_to_all | solution.py:162
  18.4 0.0 copy-done.2
  18.4 0.0 copy-start
  18.4 0.0 copy-start.1
  18.4 0.0 copy-start.3
  18.4 0.1 shard_map.65
  18.5 11.3 %all_to_all.16.came_ref = bf16[8,16,512]{2,1,0:T(8,128)(2,1)S(1)} all-to-all(bf16[8,16,512]{2,1,0:T(8,128)(2,1)S(1)} %get-tuple-element.14), channel_id=1, replica_groups={{256,0,384,128,320,64,448,192},{264,8,392,136,328,72,456,200},{272,16,4..., dimensions={0} | all-to-all | bytes 262144 | tf_op jit(solution)/shard_map/all_to_all | solution.py:166
  29.8 0.0 copy-done
  29.8 0.0 copy-done.1
  29.8 0.0 copy-done.3
  29.8 1.2 %shard_map.66 = (bf16[4,128,512]{2,1,0:T(8,128)(2,1)S(1)}, bf16[128,512]{1,0:T(8,128)(2,1)S(1)}) custom-call(bf16[8,16,512]{2,1,0:T(8,128)(2,1)S(1)} %all_to_all.16.came_ref, f32[16,512]{1,0:T(8,128)S(1)} %get-tuple-element.15.prior_ref, f32[16,8,512]{2,1,0:T(8,128)S(1)} %get-tuple-element.16.before_ref, f32[16,8,512]{2,1,0:T(8,128)S(1)} %get-tuple-element.17.fade_ref, ...), custom_call_target="tpu_custom_call" | custom-call | flops 300000000 | bytes 3000000 | tf_op jit(solution)/shard_map/pallas_call | solution.py:168
  31.0 4.6 %collective-permute-start = (bf16[4,128,512]{2,1,0:T(8,128)(2,1)S(1)}, bf16[4,128,512]{2,1,0:T(8,128)(2,1)S(1)}, u32[]{:S(2)}, u32[]{:S(2)}) collective-permute-start(bf16[4,128,512]{2,1,0:T(8,128)(2,1)S(1)} %get-tuple-element.20), channel_id=1, source_target_pairs={{0,1},{1,0},{2,3},{3,2},{4,5},{5,4},{6,7},{7,6},{8,9},{9,8},{10,11... | collective-permute-start | bytes 1572872 | tf_op jit(solution)/shard_map/ppermute | solution.py:174
  35.7 0.5 shard_map.67.kept_ref
  36.2 1.0 %collective-permute-done.came_ref = bf16[4,128,512]{2,1,0:T(8,128)(2,1)S(1)} collective-permute-done((bf16[4,128,512]{2,1,0:T(8,128)(2,1)S(1)}, bf16[4,128,512]{2,1,0:T(8,128)(2,1)S(1)}, u32[]{:S(2)}, u32[]{:S(2)}) %collective-permute-start) | collective-permute-done | bytes 524320 | tf_op jit(solution)/shard_map/ppermute | solution.py:174
  37.2 0.1 shard_map.68
  37.3 11.6 %all_to_all.17.came_ref = bf16[4,128,512]{2,1,0:T(8,128)(2,1)S(1)} all-to-all(bf16[4,128,512]{2,1,0:T(8,128)(2,1)S(1)} %shard_map.68), channel_id=1, replica_groups={{6,2,4,0},{7,3,5,1},{14,10,12,8},{15,11,13,9},{22,18,20,16},{23,19,21,1..., dimensions={0} | all-to-all | bytes 1048576 | tf_op jit(solution)/shard_map/all_to_all | solution.py:179
  48.9 0.7 %shard_map.69 = bf16[128,512]{1,0:T(8,128)(2,1)} custom-call(bf16[4,128,512]{2,1,0:T(8,128)(2,1)S(1)} %all_to_all.17.came_ref), custom_call_target="tpu_custom_call" | custom-call | flops 300000 | bytes 700000 | tf_op jit(solution)/shard_map/pallas_call | solution.py:180
Async XLA Ops:
  0.0 18.4 %copy-start.2 = (f32[16,512]{1,0:T(8,128)S(1)}, f32[16,512]{1,0:T(8,128)}, u32[]{:S(2)}) copy-start(f32[16,512]{1,0:T(8,128)} %rate_ref.3) | copy-start | bytes 98308
  18.4 11.4 %copy-start = (bf16[512,4096]{1,0:T(8,128)(2,1)S(1)}, bf16[512,4096]{1,0:T(8,128)(2,1)}, u32[]{:S(2)}) copy-start(bf16[512,4096]{1,0:T(8,128)(2,1)} %weight_ref.3) | copy-start | bytes 12582916
  18.4 11.4 %copy-start.1 = (bf16[128,512]{1,0:T(8,128)(2,1)S(1)}, bf16[128,512]{1,0:T(8,128)(2,1)}, u32[]{:S(2)}) copy-start(bf16[128,512]{1,0:T(8,128)(2,1)} %query_ref.1) | copy-start | bytes 393220
  18.4 11.4 %copy-start.3 = (f32[16,512]{1,0:T(8,128)S(1)}, f32[16,512]{1,0:T(8,128)}, u32[]{:S(2)}) copy-start(f32[16,512]{1,0:T(8,128)} %residue_ref.1) | copy-start | bytes 98308
  31.0 6.2 %collective-permute-start = (bf16[4,128,512]{2,1,0:T(8,128)(2,1)S(1)}, bf16[4,128,512]{2,1,0:T(8,128)(2,1)S(1)}, u32[]{:S(2)}, u32[]{:S(2)}) collective-permute-start(bf16[4,128,512]{2,1,0:T(8,128)(2,1)S(1)} %get-tuple-element.20), channel_id=1, source_target_pairs={{0,1},{1,0},{2,3},{3,2},{4,5},{5,4},{6,7},{7,6},{8,9},{9,8},{10,11... | collective-permute-start | bytes 1572872 | tf_op jit(solution)/shard_map/ppermute | solution.py:174
